TPU v7x, 256 devices: a whole 4x4x8 slice. The times are simulated.
256 devices in a mesh: section: 8 (over y, core), node: 32 (over z, x).
Axes of the slice: x: 4, y: 4, z: 8, core: 2. Of those that a mesh axis runs over, the one named last changes fastest.
Arguments:
- features_in: bfloat16 [8, 4096, 3, 256], P(None, 'node'), may hold values from -6 to 6
- filter_gate: bfloat16 [8, 2, 256, 512], P('section'), may hold values from -0.25 to 0.25
- self_mix: bfloat16 [8, 256, 256], P('section'), may hold values from -0.375 to 0.375
- hop_one_mix: bfloat16 [8, 2, 256, 256], P('section'), may hold values from -0.375 to 0.375
- hop_two_mix: bfloat16 [8, 2, 256, 256], P('section'), may hold values from -1 to 1
- skip_weight: bfloat16 [8, 256, 256], P('section'), may hold values from -0.375 to 0.375
- tile_values: bfloat16 [2, 32, 3, 128, 128], P(None, 'node'), may hold values from 0 to 0.125, as said below
- tile_columns: int32 [2, 32, 3], P(None, 'node'), may hold values from -1 to 32, as said below
- tile_counts: int32 [2, 32], P(None, 'node'), may hold values from 1 to 3
Outputs:
- skip_total: float32 [8, 32, 128, 3, 256], P(None, 'node', 'section')
Inputs may be any that keep to these rules, and one draw needn't show every extreme that they name: `tile_columns`: for each direction and row block r the 3 slots name the blocks r - 1, r and r + 1, in an order drawn; -1 and 32 name no block. `tile_values`: entries are zero or positive.
All inputs are finite; a program needn't handle non-finite values.
Results may differ from a plain program's by a relative error of at most 0.028.
Values may be sent and summed in bfloat16 or wider, within the bound.
A program may use at most 64 MiB of HBM per device.

v0:
```python
import jax
import jax.numpy as jnp
from jax import lax
from jax.sharding import PartitionSpec as P


def extended(value, sides, width):
    for axis, dim in sides:
        size, length = (lax.axis_size(axis), value.shape[dim])
        up = [(i, (i + 1) % size) for i in range(size - 1)]
        down = [(j, i) for i, j in up]
        last = lax.slice_in_dim(value, length - width, length, axis=dim)
        first = lax.slice_in_dim(value, 0, width, axis=dim)
        before = lax.ppermute(last, axis, up)
        after = lax.ppermute(first, axis, down)
        value = jnp.concatenate([before, value, after], axis=dim)
    return value


def shifted(value, axis, steps):
    count = lax.axis_size(axis)
    first, last = (max(0, -steps), min(count, count - steps))
    return lax.ppermute(value, axis, [(source, source + steps) for source in range(first, last)])


def gated_hidden(state, filter_gate, odd_layer):
    steps_len = state.shape[1]
    channels = state.shape[2]
    one_back = jnp.pad(state, ((0, 0), (1, 0), (0, 0)))[:, :steps_len]
    two_back = jnp.pad(state, ((0, 0), (2, 0), (0, 0)))[:, :steps_len]
    earlier = jnp.where(odd_layer, two_back, one_back)
    pre_act = jnp.dot(
        earlier.reshape(-1, channels), filter_gate[0, 0], preferred_element_type=jnp.float32
    )
    pre_act = pre_act + jnp.dot(
        state.reshape(-1, channels), filter_gate[0, 1], preferred_element_type=jnp.float32
    )
    return (jnp.tanh(pre_act[:, :channels]) * jax.nn.sigmoid(pre_act[:, channels:])).astype(
        jnp.bfloat16
    )


def body(
    features_in,
    filter_gate,
    self_mix,
    hop_one_mix,
    hop_two_mix,
    skip_weight,
    tile_values,
    tile_columns,
    tile_counts,
):
    micro, tile_rows, steps_len, channels = features_in.shape
    width = steps_len * channels
    skip_width = skip_weight.shape[2]
    section_index = lax.axis_index("section")
    block_index = lax.axis_index("node")
    odd_layer = section_index % 2 == 1
    tile_set = tile_values[:, 0].astype(jnp.float32)
    slot_ids = jnp.arange(tile_set.shape[1], dtype=jnp.int32)
    live_mask = (slot_ids[None, :] < tile_counts[:, 0][:, None]).astype(jnp.float32)
    position = tile_columns[:, 0] - block_index + 1
    onehot_slots = (position[:, :, None] == jnp.arange(3, dtype=jnp.int32)[None, None, :]).astype(
        jnp.float32
    ) * live_mask[:, :, None]
    window_tiles = jnp.einsum(
        "dks,dkij->disj", onehot_slots, tile_set, precision=lax.Precision.HIGHEST
    )
    window_tiles = window_tiles.reshape(2, tile_rows, 3 * tile_rows).astype(jnp.bfloat16)

    def layer_step(state):
        hidden = gated_hidden(state, filter_gate, odd_layer)
        hidden_rows = hidden.reshape(tile_rows, width)
        near_hidden = extended(hidden_rows, (("node", 0),), tile_rows)
        first_flat = jnp.dot(
            window_tiles.reshape(2 * tile_rows, 3 * tile_rows),
            near_hidden,
            preferred_element_type=jnp.float32,
        )
        first_hop = first_flat.astype(jnp.bfloat16).reshape(2, tile_rows, width)
        first_near = extended(first_hop, (("node", 1),), tile_rows)
        second_hop = jnp.einsum(
            "dij,djw->diw", window_tiles, first_near, preferred_element_type=jnp.float32
        ).astype(jnp.bfloat16)
        mixed_sum = jnp.dot(hidden, self_mix[0], preferred_element_type=jnp.float32)
        for direction in range(2):
            mixed_sum = mixed_sum + jnp.dot(
                first_hop[direction].reshape(-1, channels),
                hop_one_mix[0, direction],
                preferred_element_type=jnp.float32,
            )
            mixed_sum = mixed_sum + jnp.dot(
                second_hop[direction].reshape(-1, channels),
                hop_two_mix[0, direction],
                preferred_element_type=jnp.float32,
            )
        next_state = (state.astype(jnp.float32) + mixed_sum.reshape(state.shape)).astype(
            jnp.bfloat16
        )
        skip_term = jnp.dot(hidden, skip_weight[0], preferred_element_type=jnp.float32).reshape(
            tile_rows, steps_len, skip_width
        )
        return (next_state, skip_term)

    def tick_body(tick_index, carry):
        state, skip_acc = carry
        fresh = lax.dynamic_index_in_dim(
            features_in, jnp.clip(tick_index, 0, micro - 1), 0, keepdims=False
        )
        current = jnp.where(section_index == 0, fresh, state)
        next_state, skip_term = layer_step(current)
        micro_index = tick_index - section_index
        active = (micro_index >= 0) & (micro_index < micro)
        sample_slot = jnp.clip(micro_index, 0, micro - 1)
        earlier_sum = lax.dynamic_index_in_dim(skip_acc, sample_slot, 0, keepdims=False)
        updated = jnp.where(active, earlier_sum + skip_term, earlier_sum)
        skip_acc = lax.dynamic_update_index_in_dim(skip_acc, updated, sample_slot, 0)
        state = shifted(next_state, "section", 1)
        return (state, skip_acc)

    ticks = micro + lax.axis_size("section") - 1
    start_state = jnp.zeros((tile_rows, steps_len, channels), jnp.bfloat16)
    start_skip = jnp.zeros((micro, tile_rows, steps_len, skip_width), jnp.float32)
    final_state, skip_acc = lax.fori_loop(0, ticks, tick_body, (start_state, start_skip))
    return lax.psum_scatter(
        skip_acc.reshape(micro, 1, tile_rows, steps_len, skip_width),
        "section",
        scatter_dimension=2,
        tiled=True,
    )


def solution(mesh):
    in_specs = (
        P(None, "node", None, None),
        P("section", None, None, None),
        P("section", None, None),
        P("section", None, None, None),
        P("section", None, None, None),
        P("section", None, None),
        P(None, "node", None, None, None),
        P(None, "node", None),
        P(None, "node"),
    )
    out_specs = P(None, "node", "section", None, None)
    return jax.shard_map(body, mesh=mesh, in_specs=in_specs, out_specs=out_specs, check_vma=False)
```

profile of v0, /device:TPU:121, one launch (start us, length us, event | category | flops | bytes accessed | tf_op | source)
XLA Modules:
  0.0 733.0 jit_solution(6527968913148643801)
XLA Ops:
  11.8 669.5 %while.17 = (s32[]{:T(128)}, bf16[128,3,256]{2,1,0:T(4,128)(2,1)}, f32[8,128,3,256]{3,1,2,0:T(8,128)}, pred[]{:T(512)}, bf16[8,128,3,256]{3,1,2,0:T(8,128)(2,1)}...) while((s32[]{:T(128)}, bf16[128,3,256]{2,1,0:T(4,128)(2,1)}, ...), condition=%wide.region_1.2_spmd, body=%wide.region_0.1_spmd.sunk | while | flops 812777472 | bytes 34013812 | solution.py:125
  18.5 4.3 collective-permute-start
  31.2 5.2 collective-permute-start.2
  37.8 4.3 collective-permute-done.3
  49.0 3.3 collective-permute-done.4
  55.9 6.4 collective-permute-start.1
  65.5 3.4 collective-permute-done
  71.2 5.2 collective-permute-start.3
  81.9 3.4 collective-permute-done.2
  90.9 7.6 %collective-permute-done.4 = bf16[128,3,256]{2,1,0:T(4,128)(2,1)} collective-permute-done((bf16[128,3,256]{2,1,0:T(4,128)(2,1)S(1)}, bf16[128,3,256]{2,1,0:T(4,128)(2,1)}, u32[]{:S(2)}, u32[]{:S(2)}) %collective-permute-start.4) | collective-permute-done | bytes 196640 | tf_op jit(solution)/shard_map/while/body/eval_jaxpr/ppermute | solution.py:23
  102.1 5.0 collective-permute-start.1
  110.9 3.2 collective-permute-done
  116.3 4.9 collective-permute-start.3
  135.8 7.5 %collective-permute-done.4 = bf16[128,3,256]{2,1,0:T(4,128)(2,1)} collective-permute-done((bf16[128,3,256]{2,1,0:T(4,128)(2,1)S(1)}, bf16[128,3,256]{2,1,0:T(4,128)(2,1)}, u32[]{:S(2)}, u32[]{:S(2)}) %collective-permute-start.4) | collective-permute-done | bytes 196640 | tf_op jit(solution)/shard_map/while/body/eval_jaxpr/ppermute | solution.py:23
  146.9 5.0 collective-permute-start.1
  155.7 3.2 collective-permute-done
  161.1 4.9 collective-permute-start.3
  171.8 3.2 collective-permute-done.2
  180.6 7.5 %collective-permute-done.4 = bf16[128,3,256]{2,1,0:T(4,128)(2,1)} collective-permute-done((bf16[128,3,256]{2,1,0:T(4,128)(2,1)S(1)}, bf16[128,3,256]{2,1,0:T(4,128)(2,1)}, u32[]{:S(2)}, u32[]{:S(2)}) %collective-permute-start.4) | collective-permute-done | bytes 196640 | tf_op jit(solution)/shard_map/while/body/eval_jaxpr/ppermute | solution.py:23
  191.8 5.0 collective-permute-start.1
  200.6 3.2 collective-permute-done
  205.9 4.9 collective-permute-start.3
  225.4 7.5 %collective-permute-done.4 = bf16[128,3,256]{2,1,0:T(4,128)(2,1)} collective-permute-done((bf16[128,3,256]{2,1,0:T(4,128)(2,1)S(1)}, bf16[128,3,256]{2,1,0:T(4,128)(2,1)}, u32[]{:S(2)}, u32[]{:S(2)}) %collective-permute-start.4) | collective-permute-done | bytes 196640 | tf_op jit(solution)/shard_map/while/body/eval_jaxpr/ppermute | solution.py:23
  236.6 5.0 collective-permute-start.1
  245.4 3.2 collective-permute-done
  250.7 4.9 collective-permute-start.3
  270.3 7.5 %collective-permute-done.4 = bf16[128,3,256]{2,1,0:T(4,128)(2,1)} collective-permute-done((bf16[128,3,256]{2,1,0:T(4,128)(2,1)S(1)}, bf16[128,3,256]{2,1,0:T(4,128)(2,1)}, u32[]{:S(2)}, u32[]{:S(2)}) %collective-permute-start.4) | collective-permute-done | bytes 196640 | tf_op jit(solution)/shard_map/while/body/eval_jaxpr/ppermute | solution.py:23
  281.4 5.0 collective-permute-start.1
  290.2 3.2 collective-permute-done
  295.6 4.9 collective-permute-start.3
  315.1 7.5 %collective-permute-done.4 = bf16[128,3,256]{2,1,0:T(4,128)(2,1)} collective-permute-done((bf16[128,3,256]{2,1,0:T(4,128)(2,1)S(1)}, bf16[128,3,256]{2,1,0:T(4,128)(2,1)}, u32[]{:S(2)}, u32[]{:S(2)}) %collective-permute-start.4) | collective-permute-done | bytes 196640 | tf_op jit(solution)/shard_map/while/body/eval_jaxpr/ppermute | solution.py:23
  326.2 5.0 collective-permute-start.1
  335.0 3.2 collective-permute-done
  340.4 4.9 collective-permute-start.3
  359.9 7.5 %collective-permute-done.4 = bf16[128,3,256]{2,1,0:T(4,128)(2,1)} collective-permute-done((bf16[128,3,256]{2,1,0:T(4,128)(2,1)S(1)}, bf16[128,3,256]{2,1,0:T(4,128)(2,1)}, u32[]{:S(2)}, u32[]{:S(2)}) %collective-permute-start.4) | collective-permute-done | bytes 196640 | tf_op jit(solution)/shard_map/while/body/eval_jaxpr/ppermute | solution.py:23
  371.1 5.0 collective-permute-start.1
  379.9 3.2 collective-permute-done
  385.2 4.9 collective-permute-start.3
  404.7 7.5 %collective-permute-done.4 = bf16[128,3,256]{2,1,0:T(4,128)(2,1)} collective-permute-done((bf16[128,3,256]{2,1,0:T(4,128)(2,1)S(1)}, bf16[128,3,256]{2,1,0:T(4,128)(2,1)}, u32[]{:S(2)}, u32[]{:S(2)}) %collective-permute-start.4) | collective-permute-done | bytes 196640 | tf_op jit(solution)/shard_map/while/body/eval_jaxpr/ppermute | solution.py:23
  415.9 5.0 collective-permute-start.1
  424.7 3.2 collective-permute-done
  430.0 4.9 collective-permute-start.3
  449.6 7.5 %collective-permute-done.4 = bf16[128,3,256]{2,1,0:T(4,128)(2,1)} collective-permute-done((bf16[128,3,256]{2,1,0:T(4,128)(2,1)S(1)}, bf16[128,3,256]{2,1,0:T(4,128)(2,1)}, u32[]{:S(2)}, u32[]{:S(2)}) %collective-permute-start.4) | collective-permute-done | bytes 196640 | tf_op jit(solution)/shard_map/while/body/eval_jaxpr/ppermute | solution.py:23
  460.7 5.0 collective-permute-start.1
  469.5 3.2 collective-permute-done
  474.9 4.9 collective-permute-start.3
  494.4 7.5 %collective-permute-done.4 = bf16[128,3,256]{2,1,0:T(4,128)(2,1)} collective-permute-done((bf16[128,3,256]{2,1,0:T(4,128)(2,1)S(1)}, bf16[128,3,256]{2,1,0:T(4,128)(2,1)}, u32[]{:S(2)}, u32[]{:S(2)}) %collective-permute-start.4) | collective-permute-done | bytes 196640 | tf_op jit(solution)/shard_map/while/body/eval_jaxpr/ppermute | solution.py:23
  505.5 5.0 collective-permute-start.1
  514.3 3.2 collective-permute-done
  519.7 4.9 collective-permute-start.3
  539.2 7.5 %collective-permute-done.4 = bf16[128,3,256]{2,1,0:T(4,128)(2,1)} collective-permute-done((bf16[128,3,256]{2,1,0:T(4,128)(2,1)S(1)}, bf16[128,3,256]{2,1,0:T(4,128)(2,1)}, u32[]{:S(2)}, u32[]{:S(2)}) %collective-permute-start.4) | collective-permute-done | bytes 196640 | tf_op jit(solution)/shard_map/while/body/eval_jaxpr/ppermute | solution.py:23
  550.4 5.0 collective-permute-start.1
  559.2 3.2 collective-permute-done
  564.5 4.9 collective-permute-start.3
  584.0 7.5 %collective-permute-done.4 = bf16[128,3,256]{2,1,0:T(4,128)(2,1)} collective-permute-done((bf16[128,3,256]{2,1,0:T(4,128)(2,1)S(1)}, bf16[128,3,256]{2,1,0:T(4,128)(2,1)}, u32[]{:S(2)}, u32[]{:S(2)}) %collective-permute-start.4) | collective-permute-done | bytes 196640 | tf_op jit(solution)/shard_map/while/body/eval_jaxpr/ppermute | solution.py:23
  595.2 5.0 collective-permute-start.1
  604.0 3.2 collective-permute-done
  609.3 4.9 collective-permute-start.3
  628.9 7.5 %collective-permute-done.4 = bf16[128,3,256]{2,1,0:T(4,128)(2,1)} collective-permute-done((bf16[128,3,256]{2,1,0:T(4,128)(2,1)S(1)}, bf16[128,3,256]{2,1,0:T(4,128)(2,1)}, u32[]{:S(2)}, u32[]{:S(2)}) %collective-permute-start.4) | collective-permute-done | bytes 196640 | tf_op jit(solution)/shard_map/while/body/eval_jaxpr/ppermute | solution.py:23
  640.0 5.0 collective-permute-start.1
  648.8 3.2 collective-permute-done
  654.2 4.9 collective-permute-start.3
  673.7 7.5 %collective-permute-done.4 = bf16[128,3,256]{2,1,0:T(4,128)(2,1)} collective-permute-done((bf16[128,3,256]{2,1,0:T(4,128)(2,1)S(1)}, bf16[128,3,256]{2,1,0:T(4,128)(2,1)}, u32[]{:S(2)}, u32[]{:S(2)}) %collective-permute-start.4) | collective-permute-done | bytes 196640 | tf_op jit(solution)/shard_map/while/body/eval_jaxpr/ppermute | solution.py:23
  681.3 44.9 %reduce-scatter.2.cloned.1.call-done = f32[8,1,16,3,256]{4,2,3,1,0:T(8,128)} async-done(((f32[8,1,128,3,256]{4,2,3,1,0:T(8,128)}), f32[8,1,16,3,256]{4,2,3,1,0:T(8,128)}) %reduce-scatter.2.cloned.1.call-update) | async-done | bytes 393232 | tf_op jit(solution)/shard_map/reduce_scatter | solution.py:126
  (735 shorter events, 356.8 us)
Async XLA Ops:
  6.5 719.7 %reduce-scatter.2.cloned.1.call-start = ((), (), s32[]{:S(2)}) async-start(), calls=%async_computation.1 | async-start | bytes 3538944 | tf_op jit(solution)/shard_map/reduce_scatter | solution.py:126
  15.4 9.8 %collective-permute-start.1 = (bf16[128,768]{1,0:T(8,128)(2,1)S(1)}, bf16[128,768]{1,0:T(8,128)(2,1)S(1)}, u32[]{:S(2)}, u32[]{:S(2)}) collective-permute-start(bf16[128,768]{1,0:T(8,128)(2,1)S(1)} %reshape.120), channel_id=1, source_target_pairs={{0,1},{1,2},{2,3},{3,4},{4,5},{5,6},{6,7},{7,8},{8,9},{9,10},{10,1... | collective-permute-start | bytes 589832 | tf_op jit(solution)/shard_map/while/body/eval_jaxpr/ppermute | solution.py:14
  18.5 7.5 %collective-permute-start = (bf16[128,768]{1,0:T(8,128)(2,1)S(1)}, bf16[128,768]{1,0:T(8,128)(2,1)S(1)}, u32[]{:S(2)}, u32[]{:S(2)}) collective-permute-start(bf16[128,768]{1,0:T(8,128)(2,1)S(1)} %reshape.120), channel_id=1, source_target_pairs={{1,0},{2,1},{3,2},{4,3},{5,4},{6,5},{7,6},{8,7},{9,8},{10,9},{11,1... | collective-permute-start | bytes 589832 | tf_op jit(solution)/shard_map/while/body/eval_jaxpr/ppermute | solution.py:15
  28.2 13.9 %collective-permute-start.3 = (bf16[2,128,768]{1,2,0:T(8,128)(2,1)S(1)}, bf16[2,128,768]{1,2,0:T(8,128)(2,1)}, u32[]{:S(2)}, u32[]{:S(2)}) collective-permute-start(bf16[2,128,768]{1,2,0:T(8,128)(2,1)S(1)} %copy.42), channel_id=1, source_target_pairs={{0,1},{1,2},{2,3},{3,4},{4,5},{5,6},{6,7},{7,8},{8,9},{9,10},{10,1... | collective-permute-start | bytes 1179656 | tf_op jit(solution)/shard_map/while/body/eval_jaxpr/ppermute | solution.py:14
  31.2 12.2 %collective-permute-start.2 = (bf16[2,128,768]{1,2,0:T(8,128)(2,1)S(1)}, bf16[2,128,768]{1,2,0:T(8,128)(2,1)}, u32[]{:S(2)}, u32[]{:S(2)}) collective-permute-start(bf16[2,128,768]{1,2,0:T(8,128)(2,1)S(1)} %copy.42), channel_id=1, source_target_pairs={{1,0},{2,1},{3,2},{4,3},{5,4},{6,5},{7,6},{8,7},{9,8},{10,9},{11,1... | collective-permute-start | bytes 1179656 | tf_op jit(solution)/shard_map/while/body/eval_jaxpr/ppermute | solution.py:15
  55.9 9.6 %collective-permute-start.1 = (bf16[128,768]{1,0:T(8,128)(2,1)S(1)}, bf16[128,768]{1,0:T(8,128)(2,1)S(1)}, u32[]{:S(2)}, u32[]{:S(2)}) collective-permute-start(bf16[128,768]{1,0:T(8,128)(2,1)S(1)} %reshape.120), channel_id=1, source_target_pairs={{0,1},{1,2},{2,3},{3,4},{4,5},{5,6},{6,7},{7,8},{8,9},{9,10},{10,1... | collective-permute-start | bytes 589832 | tf_op jit(solution)/shard_map/while/body/eval_jaxpr/ppermute | solution.py:14
  71.2 10.7 %collective-permute-start.3 = (bf16[2,128,768]{1,2,0:T(8,128)(2,1)S(1)}, bf16[2,128,768]{1,2,0:T(8,128)(2,1)}, u32[]{:S(2)}, u32[]{:S(2)}) collective-permute-start(bf16[2,128,768]{1,2,0:T(8,128)(2,1)S(1)} %copy.42), channel_id=1, source_target_pairs={{0,1},{1,2},{2,3},{3,4},{4,5},{5,6},{6,7},{7,8},{8,9},{9,10},{10,1... | collective-permute-start | bytes 1179656 | tf_op jit(solution)/shard_map/while/body/eval_jaxpr/ppermute | solution.py:14
  76.4 8.9 %collective-permute-start.2 = (bf16[2,128,768]{1,2,0:T(8,128)(2,1)S(1)}, bf16[2,128,768]{1,2,0:T(8,128)(2,1)}, u32[]{:S(2)}, u32[]{:S(2)}) collective-permute-start(bf16[2,128,768]{1,2,0:T(8,128)(2,1)S(1)} %copy.42), channel_id=1, source_target_pairs={{1,0},{2,1},{3,2},{4,3},{5,4},{6,5},{7,6},{8,7},{9,8},{10,9},{11,1... | collective-permute-start | bytes 1179656 | tf_op jit(solution)/shard_map/while/body/eval_jaxpr/ppermute | solution.py:15
  88.6 9.8 %collective-permute-start.4 = (bf16[128,3,256]{2,1,0:T(4,128)(2,1)S(1)}, bf16[128,3,256]{2,1,0:T(4,128)(2,1)}, u32[]{:S(2)}, u32[]{:S(2)}) collective-permute-start(bf16[128,3,256]{2,1,0:T(4,128)(2,1)S(1)} %add_convert_fusion.2), channel_id=1, source_target_pairs={{0,32},{32,64},{64,96},{96,128},{128,160},{160,192},{192,224},{1,3... | collective-permute-start | bytes 589832 | tf_op jit(solution)/shard_map/while/body/eval_jaxpr/ppermute | solution.py:23
  102.1 8.8 %collective-permute-start.1 = (bf16[128,768]{1,0:T(8,128)(2,1)S(1)}, bf16[128,768]{1,0:T(8,128)(2,1)S(1)}, u32[]{:S(2)}, u32[]{:S(2)}) collective-permute-start(bf16[128,768]{1,0:T(8,128)(2,1)S(1)} %reshape.120), channel_id=1, source_target_pairs={{0,1},{1,2},{2,3},{3,4},{4,5},{5,6},{6,7},{7,8},{8,9},{9,10},{10,1... | collective-permute-start | bytes 589832 | tf_op jit(solution)/shard_map/while/body/eval_jaxpr/ppermute | solution.py:14
  107.1 7.0 collective-permute-start
  116.3 10.7 %collective-permute-start.3 = (bf16[2,128,768]{1,2,0:T(8,128)(2,1)S(1)}, bf16[2,128,768]{1,2,0:T(8,128)(2,1)}, u32[]{:S(2)}, u32[]{:S(2)}) collective-permute-start(bf16[2,128,768]{1,2,0:T(8,128)(2,1)S(1)} %copy.42), channel_id=1, source_target_pairs={{0,1},{1,2},{2,3},{3,4},{4,5},{5,6},{6,7},{7,8},{8,9},{9,10},{10,1... | collective-permute-start | bytes 1179656 | tf_op jit(solution)/shard_map/while/body/eval_jaxpr/ppermute | solution.py:14
  121.2 9.0 %collective-permute-start.2 = (bf16[2,128,768]{1,2,0:T(8,128)(2,1)S(1)}, bf16[2,128,768]{1,2,0:T(8,128)(2,1)}, u32[]{:S(2)}, u32[]{:S(2)}) collective-permute-start(bf16[2,128,768]{1,2,0:T(8,128)(2,1)S(1)} %copy.42), channel_id=1, source_target_pairs={{1,0},{2,1},{3,2},{4,3},{5,4},{6,5},{7,6},{8,7},{9,8},{10,9},{11,1... | collective-permute-start | bytes 1179656 | tf_op jit(solution)/shard_map/while/body/eval_jaxpr/ppermute | solution.py:15
  133.5 9.8 %collective-permute-start.4 = (bf16[128,3,256]{2,1,0:T(4,128)(2,1)S(1)}, bf16[128,3,256]{2,1,0:T(4,128)(2,1)}, u32[]{:S(2)}, u32[]{:S(2)}) collective-permute-start(bf16[128,3,256]{2,1,0:T(4,128)(2,1)S(1)} %add_convert_fusion.2), channel_id=1, source_target_pairs={{0,32},{32,64},{64,96},{96,128},{128,160},{160,192},{192,224},{1,3... | collective-permute-start | bytes 589832 | tf_op jit(solution)/shard_map/while/body/eval_jaxpr/ppermute | solution.py:23
  146.9 8.8 %collective-permute-start.1 = (bf16[128,768]{1,0:T(8,128)(2,1)S(1)}, bf16[128,768]{1,0:T(8,128)(2,1)S(1)}, u32[]{:S(2)}, u32[]{:S(2)}) collective-permute-start(bf16[128,768]{1,0:T(8,128)(2,1)S(1)} %reshape.120), channel_id=1, source_target_pairs={{0,1},{1,2},{2,3},{3,4},{4,5},{5,6},{6,7},{7,8},{8,9},{9,10},{10,1... | collective-permute-start | bytes 589832 | tf_op jit(solution)/shard_map/while/body/eval_jaxpr/ppermute | solution.py:14
  161.1 10.7 %collective-permute-start.3 = (bf16[2,128,768]{1,2,0:T(8,128)(2,1)S(1)}, bf16[2,128,768]{1,2,0:T(8,128)(2,1)}, u32[]{:S(2)}, u32[]{:S(2)}) collective-permute-start(bf16[2,128,768]{1,2,0:T(8,128)(2,1)S(1)} %copy.42), channel_id=1, source_target_pairs={{0,1},{1,2},{2,3},{3,4},{4,5},{5,6},{6,7},{7,8},{8,9},{9,10},{10,1... | collective-permute-start | bytes 1179656 | tf_op jit(solution)/shard_map/while/body/eval_jaxpr/ppermute | solution.py:14
  166.0 9.0 %collective-permute-start.2 = (bf16[2,128,768]{1,2,0:T(8,128)(2,1)S(1)}, bf16[2,128,768]{1,2,0:T(8,128)(2,1)}, u32[]{:S(2)}, u32[]{:S(2)}) collective-permute-start(bf16[2,128,768]{1,2,0:T(8,128)(2,1)S(1)} %copy.42), channel_id=1, source_target_pairs={{1,0},{2,1},{3,2},{4,3},{5,4},{6,5},{7,6},{8,7},{9,8},{10,9},{11,1... | collective-permute-start | bytes 1179656 | tf_op jit(solution)/shard_map/while/body/eval_jaxpr/ppermute | solution.py:15
  178.3 9.8 %collective-permute-start.4 = (bf16[128,3,256]{2,1,0:T(4,128)(2,1)S(1)}, bf16[128,3,256]{2,1,0:T(4,128)(2,1)}, u32[]{:S(2)}, u32[]{:S(2)}) collective-permute-start(bf16[128,3,256]{2,1,0:T(4,128)(2,1)S(1)} %add_convert_fusion.2), channel_id=1, source_target_pairs={{0,32},{32,64},{64,96},{96,128},{128,160},{160,192},{192,224},{1,3... | collective-permute-start | bytes 589832 | tf_op jit(solution)/shard_map/while/body/eval_jaxpr/ppermute | solution.py:23
  191.8 8.8 %collective-permute-start.1 = (bf16[128,768]{1,0:T(8,128)(2,1)S(1)}, bf16[128,768]{1,0:T(8,128)(2,1)S(1)}, u32[]{:S(2)}, u32[]{:S(2)}) collective-permute-start(bf16[128,768]{1,0:T(8,128)(2,1)S(1)} %reshape.120), channel_id=1, source_target_pairs={{0,1},{1,2},{2,3},{3,4},{4,5},{5,6},{6,7},{7,8},{8,9},{9,10},{10,1... | collective-permute-start | bytes 589832 | tf_op jit(solution)/shard_map/while/body/eval_jaxpr/ppermute | solution.py:14
  205.9 10.7 %collective-permute-start.3 = (bf16[2,128,768]{1,2,0:T(8,128)(2,1)S(1)}, bf16[2,128,768]{1,2,0:T(8,128)(2,1)}, u32[]{:S(2)}, u32[]{:S(2)}) collective-permute-start(bf16[2,128,768]{1,2,0:T(8,128)(2,1)S(1)} %copy.42), channel_id=1, source_target_pairs={{0,1},{1,2},{2,3},{3,4},{4,5},{5,6},{6,7},{7,8},{8,9},{9,10},{10,1... | collective-permute-start | bytes 1179656 | tf_op jit(solution)/shard_map/while/body/eval_jaxpr/ppermute | solution.py:14
  210.8 9.0 %collective-permute-start.2 = (bf16[2,128,768]{1,2,0:T(8,128)(2,1)S(1)}, bf16[2,128,768]{1,2,0:T(8,128)(2,1)}, u32[]{:S(2)}, u32[]{:S(2)}) collective-permute-start(bf16[2,128,768]{1,2,0:T(8,128)(2,1)S(1)} %copy.42), channel_id=1, source_target_pairs={{1,0},{2,1},{3,2},{4,3},{5,4},{6,5},{7,6},{8,7},{9,8},{10,9},{11,1... | collective-permute-start | bytes 1179656 | tf_op jit(solution)/shard_map/while/body/eval_jaxpr/ppermute | solution.py:15
  223.2 9.8 %collective-permute-start.4 = (bf16[128,3,256]{2,1,0:T(4,128)(2,1)S(1)}, bf16[128,3,256]{2,1,0:T(4,128)(2,1)}, u32[]{:S(2)}, u32[]{:S(2)}) collective-permute-start(bf16[128,3,256]{2,1,0:T(4,128)(2,1)S(1)} %add_convert_fusion.2), channel_id=1, source_target_pairs={{0,32},{32,64},{64,96},{96,128},{128,160},{160,192},{192,224},{1,3... | collective-permute-start | bytes 589832 | tf_op jit(solution)/shard_map/while/body/eval_jaxpr/ppermute | solution.py:23
  236.6 8.8 %collective-permute-start.1 = (bf16[128,768]{1,0:T(8,128)(2,1)S(1)}, bf16[128,768]{1,0:T(8,128)(2,1)S(1)}, u32[]{:S(2)}, u32[]{:S(2)}) collective-permute-start(bf16[128,768]{1,0:T(8,128)(2,1)S(1)} %reshape.120), channel_id=1, source_target_pairs={{0,1},{1,2},{2,3},{3,4},{4,5},{5,6},{6,7},{7,8},{8,9},{9,10},{10,1... | collective-permute-start | bytes 589832 | tf_op jit(solution)/shard_map/while/body/eval_jaxpr/ppermute | solution.py:14
  241.6 7.0 collective-permute-start
  250.7 10.7 %collective-permute-start.3 = (bf16[2,128,768]{1,2,0:T(8,128)(2,1)S(1)}, bf16[2,128,768]{1,2,0:T(8,128)(2,1)}, u32[]{:S(2)}, u32[]{:S(2)}) collective-permute-start(bf16[2,128,768]{1,2,0:T(8,128)(2,1)S(1)} %copy.42), channel_id=1, source_target_pairs={{0,1},{1,2},{2,3},{3,4},{4,5},{5,6},{6,7},{7,8},{8,9},{9,10},{10,1... | collective-permute-start | bytes 1179656 | tf_op jit(solution)/shard_map/while/body/eval_jaxpr/ppermute | solution.py:14
  255.7 9.0 %collective-permute-start.2 = (bf16[2,128,768]{1,2,0:T(8,128)(2,1)S(1)}, bf16[2,128,768]{1,2,0:T(8,128)(2,1)}, u32[]{:S(2)}, u32[]{:S(2)}) collective-permute-start(bf16[2,128,768]{1,2,0:T(8,128)(2,1)S(1)} %copy.42), channel_id=1, source_target_pairs={{1,0},{2,1},{3,2},{4,3},{5,4},{6,5},{7,6},{8,7},{9,8},{10,9},{11,1... | collective-permute-start | bytes 1179656 | tf_op jit(solution)/shard_map/while/body/eval_jaxpr/ppermute | solution.py:15
  268.0 9.8 %collective-permute-start.4 = (bf16[128,3,256]{2,1,0:T(4,128)(2,1)S(1)}, bf16[128,3,256]{2,1,0:T(4,128)(2,1)}, u32[]{:S(2)}, u32[]{:S(2)}) collective-permute-start(bf16[128,3,256]{2,1,0:T(4,128)(2,1)S(1)} %add_convert_fusion.2), channel_id=1, source_target_pairs={{0,32},{32,64},{64,96},{96,128},{128,160},{160,192},{192,224},{1,3... | collective-permute-start | bytes 589832 | tf_op jit(solution)/shard_map/while/body/eval_jaxpr/ppermute | solution.py:23
  281.4 8.8 %collective-permute-start.1 = (bf16[128,768]{1,0:T(8,128)(2,1)S(1)}, bf16[128,768]{1,0:T(8,128)(2,1)S(1)}, u32[]{:S(2)}, u32[]{:S(2)}) collective-permute-start(bf16[128,768]{1,0:T(8,128)(2,1)S(1)} %reshape.120), channel_id=1, source_target_pairs={{0,1},{1,2},{2,3},{3,4},{4,5},{5,6},{6,7},{7,8},{8,9},{9,10},{10,1... | collective-permute-start | bytes 589832 | tf_op jit(solution)/shard_map/while/body/eval_jaxpr/ppermute | solution.py:14
  286.4 7.0 collective-permute-start
  295.6 10.7 %collective-permute-start.3 = (bf16[2,128,768]{1,2,0:T(8,128)(2,1)S(1)}, bf16[2,128,768]{1,2,0:T(8,128)(2,1)}, u32[]{:S(2)}, u32[]{:S(2)}) collective-permute-start(bf16[2,128,768]{1,2,0:T(8,128)(2,1)S(1)} %copy.42), channel_id=1, source_target_pairs={{0,1},{1,2},{2,3},{3,4},{4,5},{5,6},{6,7},{7,8},{8,9},{9,10},{10,1... | collective-permute-start | bytes 1179656 | tf_op jit(solution)/shard_map/while/body/eval_jaxpr/ppermute | solution.py:14
  300.5 9.0 %collective-permute-start.2 = (bf16[2,128,768]{1,2,0:T(8,128)(2,1)S(1)}, bf16[2,128,768]{1,2,0:T(8,128)(2,1)}, u32[]{:S(2)}, u32[]{:S(2)}) collective-permute-start(bf16[2,128,768]{1,2,0:T(8,128)(2,1)S(1)} %copy.42), channel_id=1, source_target_pairs={{1,0},{2,1},{3,2},{4,3},{5,4},{6,5},{7,6},{8,7},{9,8},{10,9},{11,1... | collective-permute-start | bytes 1179656 | tf_op jit(solution)/shard_map/while/body/eval_jaxpr/ppermute | solution.py:15
  312.8 9.8 %collective-permute-start.4 = (bf16[128,3,256]{2,1,0:T(4,128)(2,1)S(1)}, bf16[128,3,256]{2,1,0:T(4,128)(2,1)}, u32[]{:S(2)}, u32[]{:S(2)}) collective-permute-start(bf16[128,3,256]{2,1,0:T(4,128)(2,1)S(1)} %add_convert_fusion.2), channel_id=1, source_target_pairs={{0,32},{32,64},{64,96},{96,128},{128,160},{160,192},{192,224},{1,3... | collective-permute-start | bytes 589832 | tf_op jit(solution)/shard_map/while/body/eval_jaxpr/ppermute | solution.py:23
  326.2 8.8 %collective-permute-start.1 = (bf16[128,768]{1,0:T(8,128)(2,1)S(1)}, bf16[128,768]{1,0:T(8,128)(2,1)S(1)}, u32[]{:S(2)}, u32[]{:S(2)}) collective-permute-start(bf16[128,768]{1,0:T(8,128)(2,1)S(1)} %reshape.120), channel_id=1, source_target_pairs={{0,1},{1,2},{2,3},{3,4},{4,5},{5,6},{6,7},{7,8},{8,9},{9,10},{10,1... | collective-permute-start | bytes 589832 | tf_op jit(solution)/shard_map/while/body/eval_jaxpr/ppermute | solution.py:14
  340.4 10.7 %collective-permute-start.3 = (bf16[2,128,768]{1,2,0:T(8,128)(2,1)S(1)}, bf16[2,128,768]{1,2,0:T(8,128)(2,1)}, u32[]{:S(2)}, u32[]{:S(2)}) collective-permute-start(bf16[2,128,768]{1,2,0:T(8,128)(2,1)S(1)} %copy.42), channel_id=1, source_target_pairs={{0,1},{1,2},{2,3},{3,4},{4,5},{5,6},{6,7},{7,8},{8,9},{9,10},{10,1... | collective-permute-start | bytes 1179656 | tf_op jit(solution)/shard_map/while/body/eval_jaxpr/ppermute | solution.py:14
  345.3 9.0 %collective-permute-start.2 = (bf16[2,128,768]{1,2,0:T(8,128)(2,1)S(1)}, bf16[2,128,768]{1,2,0:T(8,128)(2,1)}, u32[]{:S(2)}, u32[]{:S(2)}) collective-permute-start(bf16[2,128,768]{1,2,0:T(8,128)(2,1)S(1)} %copy.42), channel_id=1, source_target_pairs={{1,0},{2,1},{3,2},{4,3},{5,4},{6,5},{7,6},{8,7},{9,8},{10,9},{11,1... | collective-permute-start | bytes 1179656 | tf_op jit(solution)/shard_map/while/body/eval_jaxpr/ppermute | solution.py:15
  357.6 9.8 %collective-permute-start.4 = (bf16[128,3,256]{2,1,0:T(4,128)(2,1)S(1)}, bf16[128,3,256]{2,1,0:T(4,128)(2,1)}, u32[]{:S(2)}, u32[]{:S(2)}) collective-permute-start(bf16[128,3,256]{2,1,0:T(4,128)(2,1)S(1)} %add_convert_fusion.2), channel_id=1, source_target_pairs={{0,32},{32,64},{64,96},{96,128},{128,160},{160,192},{192,224},{1,3... | collective-permute-start | bytes 589832 | tf_op jit(solution)/shard_map/while/body/eval_jaxpr/ppermute | solution.py:23
  371.1 8.8 %collective-permute-start.1 = (bf16[128,768]{1,0:T(8,128)(2,1)S(1)}, bf16[128,768]{1,0:T(8,128)(2,1)S(1)}, u32[]{:S(2)}, u32[]{:S(2)}) collective-permute-start(bf16[128,768]{1,0:T(8,128)(2,1)S(1)} %reshape.120), channel_id=1, source_target_pairs={{0,1},{1,2},{2,3},{3,4},{4,5},{5,6},{6,7},{7,8},{8,9},{9,10},{10,1... | collective-permute-start | bytes 589832 | tf_op jit(solution)/shard_map/while/body/eval_jaxpr/ppermute | solution.py:14
  385.2 10.7 %collective-permute-start.3 = (bf16[2,128,768]{1,2,0:T(8,128)(2,1)S(1)}, bf16[2,128,768]{1,2,0:T(8,128)(2,1)}, u32[]{:S(2)}, u32[]{:S(2)}) collective-permute-start(bf16[2,128,768]{1,2,0:T(8,128)(2,1)S(1)} %copy.42), channel_id=1, source_target_pairs={{0,1},{1,2},{2,3},{3,4},{4,5},{5,6},{6,7},{7,8},{8,9},{9,10},{10,1... | collective-permute-start | bytes 1179656 | tf_op jit(solution)/shard_map/while/body/eval_jaxpr/ppermute | solution.py:14
  390.2 9.0 %collective-permute-start.2 = (bf16[2,128,768]{1,2,0:T(8,128)(2,1)S(1)}, bf16[2,128,768]{1,2,0:T(8,128)(2,1)}, u32[]{:S(2)}, u32[]{:S(2)}) collective-permute-start(bf16[2,128,768]{1,2,0:T(8,128)(2,1)S(1)} %copy.42), channel_id=1, source_target_pairs={{1,0},{2,1},{3,2},{4,3},{5,4},{6,5},{7,6},{8,7},{9,8},{10,9},{11,1... | collective-permute-start | bytes 1179656 | tf_op jit(solution)/shard_map/while/body/eval_jaxpr/ppermute | solution.py:15
  402.5 9.8 %collective-permute-start.4 = (bf16[128,3,256]{2,1,0:T(4,128)(2,1)S(1)}, bf16[128,3,256]{2,1,0:T(4,128)(2,1)}, u32[]{:S(2)}, u32[]{:S(2)}) collective-permute-start(bf16[128,3,256]{2,1,0:T(4,128)(2,1)S(1)} %add_convert_fusion.2), channel_id=1, source_target_pairs={{0,32},{32,64},{64,96},{96,128},{128,160},{160,192},{192,224},{1,3... | collective-permute-start | bytes 589832 | tf_op jit(solution)/shard_map/while/body/eval_jaxpr/ppermute | solution.py:23
  415.9 8.8 %collective-permute-start.1 = (bf16[128,768]{1,0:T(8,128)(2,1)S(1)}, bf16[128,768]{1,0:T(8,128)(2,1)S(1)}, u32[]{:S(2)}, u32[]{:S(2)}) collective-permute-start(bf16[128,768]{1,0:T(8,128)(2,1)S(1)} %reshape.120), channel_id=1, source_target_pairs={{0,1},{1,2},{2,3},{3,4},{4,5},{5,6},{6,7},{7,8},{8,9},{9,10},{10,1... | collective-permute-start | bytes 589832 | tf_op jit(solution)/shard_map/while/body/eval_jaxpr/ppermute | solution.py:14
  430.0 10.7 %collective-permute-start.3 = (bf16[2,128,768]{1,2,0:T(8,128)(2,1)S(1)}, bf16[2,128,768]{1,2,0:T(8,128)(2,1)}, u32[]{:S(2)}, u32[]{:S(2)}) collective-permute-start(bf16[2,128,768]{1,2,0:T(8,128)(2,1)S(1)} %copy.42), channel_id=1, source_target_pairs={{0,1},{1,2},{2,3},{3,4},{4,5},{5,6},{6,7},{7,8},{8,9},{9,10},{10,1... | collective-permute-start | bytes 1179656 | tf_op jit(solution)/shard_map/while/body/eval_jaxpr/ppermute | solution.py:14
  435.0 9.0 %collective-permute-start.2 = (bf16[2,128,768]{1,2,0:T(8,128)(2,1)S(1)}, bf16[2,128,768]{1,2,0:T(8,128)(2,1)}, u32[]{:S(2)}, u32[]{:S(2)}) collective-permute-start(bf16[2,128,768]{1,2,0:T(8,128)(2,1)S(1)} %copy.42), channel_id=1, source_target_pairs={{1,0},{2,1},{3,2},{4,3},{5,4},{6,5},{7,6},{8,7},{9,8},{10,9},{11,1... | collective-permute-start | bytes 1179656 | tf_op jit(solution)/shard_map/while/body/eval_jaxpr/ppermute | solution.py:15
  447.3 9.8 %collective-permute-start.4 = (bf16[128,3,256]{2,1,0:T(4,128)(2,1)S(1)}, bf16[128,3,256]{2,1,0:T(4,128)(2,1)}, u32[]{:S(2)}, u32[]{:S(2)}) collective-permute-start(bf16[128,3,256]{2,1,0:T(4,128)(2,1)S(1)} %add_convert_fusion.2), channel_id=1, source_target_pairs={{0,32},{32,64},{64,96},{96,128},{128,160},{160,192},{192,224},{1,3... | collective-permute-start | bytes 589832 | tf_op jit(solution)/shard_map/while/body/eval_jaxpr/ppermute | solution.py:23
  460.7 8.8 %collective-permute-start.1 = (bf16[128,768]{1,0:T(8,128)(2,1)S(1)}, bf16[128,768]{1,0:T(8,128)(2,1)S(1)}, u32[]{:S(2)}, u32[]{:S(2)}) collective-permute-start(bf16[128,768]{1,0:T(8,128)(2,1)S(1)} %reshape.120), channel_id=1, source_target_pairs={{0,1},{1,2},{2,3},{3,4},{4,5},{5,6},{6,7},{7,8},{8,9},{9,10},{10,1... | collective-permute-start | bytes 589832 | tf_op jit(solution)/shard_map/while/body/eval_jaxpr/ppermute | solution.py:14
  474.9 10.7 %collective-permute-start.3 = (bf16[2,128,768]{1,2,0:T(8,128)(2,1)S(1)}, bf16[2,128,768]{1,2,0:T(8,128)(2,1)}, u32[]{:S(2)}, u32[]{:S(2)}) collective-permute-start(bf16[2,128,768]{1,2,0:T(8,128)(2,1)S(1)} %copy.42), channel_id=1, source_target_pairs={{0,1},{1,2},{2,3},{3,4},{4,5},{5,6},{6,7},{7,8},{8,9},{9,10},{10,1... | collective-permute-start | bytes 1179656 | tf_op jit(solution)/shard_map/while/body/eval_jaxpr/ppermute | solution.py:14
  479.8 9.0 %collective-permute-start.2 = (bf16[2,128,768]{1,2,0:T(8,128)(2,1)S(1)}, bf16[2,128,768]{1,2,0:T(8,128)(2,1)}, u32[]{:S(2)}, u32[]{:S(2)}) collective-permute-start(bf16[2,128,768]{1,2,0:T(8,128)(2,1)S(1)} %copy.42), channel_id=1, source_target_pairs={{1,0},{2,1},{3,2},{4,3},{5,4},{6,5},{7,6},{8,7},{9,8},{10,9},{11,1... | collective-permute-start | bytes 1179656 | tf_op jit(solution)/shard_map/while/body/eval_jaxpr/ppermute | solution.py:15
  492.1 9.8 %collective-permute-start.4 = (bf16[128,3,256]{2,1,0:T(4,128)(2,1)S(1)}, bf16[128,3,256]{2,1,0:T(4,128)(2,1)}, u32[]{:S(2)}, u32[]{:S(2)}) collective-permute-start(bf16[128,3,256]{2,1,0:T(4,128)(2,1)S(1)} %add_convert_fusion.2), channel_id=1, source_target_pairs={{0,32},{32,64},{64,96},{96,128},{128,160},{160,192},{192,224},{1,3... | collective-permute-start | bytes 589832 | tf_op jit(solution)/shard_map/while/body/eval_jaxpr/ppermute | solution.py:23
  505.5 8.8 %collective-permute-start.1 = (bf16[128,768]{1,0:T(8,128)(2,1)S(1)}, bf16[128,768]{1,0:T(8,128)(2,1)S(1)}, u32[]{:S(2)}, u32[]{:S(2)}) collective-permute-start(bf16[128,768]{1,0:T(8,128)(2,1)S(1)} %reshape.120), channel_id=1, source_target_pairs={{0,1},{1,2},{2,3},{3,4},{4,5},{5,6},{6,7},{7,8},{8,9},{9,10},{10,1... | collective-permute-start | bytes 589832 | tf_op jit(solution)/shard_map/while/body/eval_jaxpr/ppermute | solution.py:14
  519.7 10.7 %collective-permute-start.3 = (bf16[2,128,768]{1,2,0:T(8,128)(2,1)S(1)}, bf16[2,128,768]{1,2,0:T(8,128)(2,1)}, u32[]{:S(2)}, u32[]{:S(2)}) collective-permute-start(bf16[2,128,768]{1,2,0:T(8,128)(2,1)S(1)} %copy.42), channel_id=1, source_target_pairs={{0,1},{1,2},{2,3},{3,4},{4,5},{5,6},{6,7},{7,8},{8,9},{9,10},{10,1... | collective-permute-start | bytes 1179656 | tf_op jit(solution)/shard_map/while/body/eval_jaxpr/ppermute | solution.py:14
  524.6 9.0 %collective-permute-start.2 = (bf16[2,128,768]{1,2,0:T(8,128)(2,1)S(1)}, bf16[2,128,768]{1,2,0:T(8,128)(2,1)}, u32[]{:S(2)}, u32[]{:S(2)}) collective-permute-start(bf16[2,128,768]{1,2,0:T(8,128)(2,1)S(1)} %copy.42), channel_id=1, source_target_pairs={{1,0},{2,1},{3,2},{4,3},{5,4},{6,5},{7,6},{8,7},{9,8},{10,9},{11,1... | collective-permute-start | bytes 1179656 | tf_op jit(solution)/shard_map/while/body/eval_jaxpr/ppermute | solution.py:15
  536.9 9.8 %collective-permute-start.4 = (bf16[128,3,256]{2,1,0:T(4,128)(2,1)S(1)}, bf16[128,3,256]{2,1,0:T(4,128)(2,1)}, u32[]{:S(2)}, u32[]{:S(2)}) collective-permute-start(bf16[128,3,256]{2,1,0:T(4,128)(2,1)S(1)} %add_convert_fusion.2), channel_id=1, source_target_pairs={{0,32},{32,64},{64,96},{96,128},{128,160},{160,192},{192,224},{1,3... | collective-permute-start | bytes 589832 | tf_op jit(solution)/shard_map/while/body/eval_jaxpr/ppermute | solution.py:23
  550.4 8.8 %collective-permute-start.1 = (bf16[128,768]{1,0:T(8,128)(2,1)S(1)}, bf16[128,768]{1,0:T(8,128)(2,1)S(1)}, u32[]{:S(2)}, u32[]{:S(2)}) collective-permute-start(bf16[128,768]{1,0:T(8,128)(2,1)S(1)} %reshape.120), channel_id=1, source_target_pairs={{0,1},{1,2},{2,3},{3,4},{4,5},{5,6},{6,7},{7,8},{8,9},{9,10},{10,1... | collective-permute-start | bytes 589832 | tf_op jit(solution)/shard_map/while/body/eval_jaxpr/ppermute | solution.py:14
  564.5 10.7 %collective-permute-start.3 = (bf16[2,128,768]{1,2,0:T(8,128)(2,1)S(1)}, bf16[2,128,768]{1,2,0:T(8,128)(2,1)}, u32[]{:S(2)}, u32[]{:S(2)}) collective-permute-start(bf16[2,128,768]{1,2,0:T(8,128)(2,1)S(1)} %copy.42), channel_id=1, source_target_pairs={{0,1},{1,2},{2,3},{3,4},{4,5},{5,6},{6,7},{7,8},{8,9},{9,10},{10,1... | collective-permute-start | bytes 1179656 | tf_op jit(solution)/shard_map/while/body/eval_jaxpr/ppermute | solution.py:14
  569.5 9.0 %collective-permute-start.2 = (bf16[2,128,768]{1,2,0:T(8,128)(2,1)S(1)}, bf16[2,128,768]{1,2,0:T(8,128)(2,1)}, u32[]{:S(2)}, u32[]{:S(2)}) collective-permute-start(bf16[2,128,768]{1,2,0:T(8,128)(2,1)S(1)} %copy.42), channel_id=1, source_target_pairs={{1,0},{2,1},{3,2},{4,3},{5,4},{6,5},{7,6},{8,7},{9,8},{10,9},{11,1... | collective-permute-start | bytes 1179656 | tf_op jit(solution)/shard_map/while/body/eval_jaxpr/ppermute | solution.py:15
  581.8 9.8 %collective-permute-start.4 = (bf16[128,3,256]{2,1,0:T(4,128)(2,1)S(1)}, bf16[128,3,256]{2,1,0:T(4,128)(2,1)}, u32[]{:S(2)}, u32[]{:S(2)}) collective-permute-start(bf16[128,3,256]{2,1,0:T(4,128)(2,1)S(1)} %add_convert_fusion.2), channel_id=1, source_target_pairs={{0,32},{32,64},{64,96},{96,128},{128,160},{160,192},{192,224},{1,3... | collective-permute-start | bytes 589832 | tf_op jit(solution)/shard_map/while/body/eval_jaxpr/ppermute | solution.py:23
  595.2 8.8 %collective-permute-start.1 = (bf16[128,768]{1,0:T(8,128)(2,1)S(1)}, bf16[128,768]{1,0:T(8,128)(2,1)S(1)}, u32[]{:S(2)}, u32[]{:S(2)}) collective-permute-start(bf16[128,768]{1,0:T(8,128)(2,1)S(1)} %reshape.120), channel_id=1, source_target_pairs={{0,1},{1,2},{2,3},{3,4},{4,5},{5,6},{6,7},{7,8},{8,9},{9,10},{10,1... | collective-permute-start | bytes 589832 | tf_op jit(solution)/shard_map/while/body/eval_jaxpr/ppermute | solution.py:14
  609.3 10.7 %collective-permute-start.3 = (bf16[2,128,768]{1,2,0:T(8,128)(2,1)S(1)}, bf16[2,128,768]{1,2,0:T(8,128)(2,1)}, u32[]{:S(2)}, u32[]{:S(2)}) collective-permute-start(bf16[2,128,768]{1,2,0:T(8,128)(2,1)S(1)} %copy.42), channel_id=1, source_target_pairs={{0,1},{1,2},{2,3},{3,4},{4,5},{5,6},{6,7},{7,8},{8,9},{9,10},{10,1... | collective-permute-start | bytes 1179656 | tf_op jit(solution)/shard_map/while/body/eval_jaxpr/ppermute | solution.py:14
  614.3 9.0 %collective-permute-start.2 = (bf16[2,128,768]{1,2,0:T(8,128)(2,1)S(1)}, bf16[2,128,768]{1,2,0:T(8,128)(2,1)}, u32[]{:S(2)}, u32[]{:S(2)}) collective-permute-start(bf16[2,128,768]{1,2,0:T(8,128)(2,1)S(1)} %copy.42), channel_id=1, source_target_pairs={{1,0},{2,1},{3,2},{4,3},{5,4},{6,5},{7,6},{8,7},{9,8},{10,9},{11,1... | collective-permute-start | bytes 1179656 | tf_op jit(solution)/shard_map/while/body/eval_jaxpr/ppermute | solution.py:15
  626.6 9.8 %collective-permute-start.4 = (bf16[128,3,256]{2,1,0:T(4,128)(2,1)S(1)}, bf16[128,3,256]{2,1,0:T(4,128)(2,1)}, u32[]{:S(2)}, u32[]{:S(2)}) collective-permute-start(bf16[128,3,256]{2,1,0:T(4,128)(2,1)S(1)} %add_convert_fusion.2), channel_id=1, source_target_pairs={{0,32},{32,64},{64,96},{96,128},{128,160},{160,192},{192,224},{1,3... | collective-permute-start | bytes 589832 | tf_op jit(solution)/shard_map/while/body/eval_jaxpr/ppermute | solution.py:23
  640.0 8.8 %collective-permute-start.1 = (bf16[128,768]{1,0:T(8,128)(2,1)S(1)}, bf16[128,768]{1,0:T(8,128)(2,1)S(1)}, u32[]{:S(2)}, u32[]{:S(2)}) collective-permute-start(bf16[128,768]{1,0:T(8,128)(2,1)S(1)} %reshape.120), channel_id=1, source_target_pairs={{0,1},{1,2},{2,3},{3,4},{4,5},{5,6},{6,7},{7,8},{8,9},{9,10},{10,1... | collective-permute-start | bytes 589832 | tf_op jit(solution)/shard_map/while/body/eval_jaxpr/ppermute | solution.py:14
  654.2 10.7 %collective-permute-start.3 = (bf16[2,128,768]{1,2,0:T(8,128)(2,1)S(1)}, bf16[2,128,768]{1,2,0:T(8,128)(2,1)}, u32[]{:S(2)}, u32[]{:S(2)}) collective-permute-start(bf16[2,128,768]{1,2,0:T(8,128)(2,1)S(1)} %copy.42), channel_id=1, source_target_pairs={{0,1},{1,2},{2,3},{3,4},{4,5},{5,6},{6,7},{7,8},{8,9},{9,10},{10,1... | collective-permute-start | bytes 1179656 | tf_op jit(solution)/shard_map/while/body/eval_jaxpr/ppermute | solution.py:14
  659.1 9.0 %collective-permute-start.2 = (bf16[2,128,768]{1,2,0:T(8,128)(2,1)S(1)}, bf16[2,128,768]{1,2,0:T(8,128)(2,1)}, u32[]{:S(2)}, u32[]{:S(2)}) collective-permute-start(bf16[2,128,768]{1,2,0:T(8,128)(2,1)S(1)} %copy.42), channel_id=1, source_target_pairs={{1,0},{2,1},{3,2},{4,3},{5,4},{6,5},{7,6},{8,7},{9,8},{10,9},{11,1... | collective-permute-start | bytes 1179656 | tf_op jit(solution)/shard_map/while/body/eval_jaxpr/ppermute | solution.py:15
  671.4 9.8 %collective-permute-start.4 = (bf16[128,3,256]{2,1,0:T(4,128)(2,1)S(1)}, bf16[128,3,256]{2,1,0:T(4,128)(2,1)}, u32[]{:S(2)}, u32[]{:S(2)}) collective-permute-start(bf16[128,3,256]{2,1,0:T(4,128)(2,1)S(1)} %add_convert_fusion.2), channel_id=1, source_target_pairs={{0,32},{32,64},{64,96},{96,128},{128,160},{160,192},{192,224},{1,3... | collective-permute-start | bytes 589832 | tf_op jit(solution)/shard_map/while/body/eval_jaxpr/ppermute | solution.py:23
  (106 other events, 772.2 us)
Sparse Core Ops, SparseCore 0:
  681.4 44.7 reduce-scatter.1
where the time goes:
time: 741 us; the launch traced here: 733 us
  waiting for transfers between devices  277 us (37%)
  starting transfers between devices  243 us (33%)
  matrix products  95.8 us (13%)
  local copies, waits for them, and re-layouts  71.7 us (10%)
  other arithmetic  27.8 us (4%)
  between operations  13.4 us (2%)
    ppermute x30, starting transfers between devices, extended(): before = lax.ppermute(last, axis, up)  146 us
    ppermute x15, waiting for transfers between devices, shifted(): lax.ppermute(value, axis, [(source, source + steps) for source in range(f...  109 us
    ppermute x30, waiting for transfers between devices, extended(): after = lax.ppermute(first, axis, down)  91.1 us
    ppermute x30, starting transfers between devices, extended(): after = lax.ppermute(first, axis, down)  77.4 us
    reduce_scatter x1, waiting for transfers between devices, body(): lax.psum_scatter(skip_acc.reshape(micro, 1, tile_rows, steps_len, skip_wi...  44.9 us
    ppermute x30, waiting for transfers between devices, extended(): before = lax.ppermute(last, axis, up)  32.6 us
    dot_general x15, matrix products, layer_step(): jnp.einsum('dij,djw->diw', window_tiles, first_near, preferred_element_ty...  24.4 us
    dot_general x30, matrix products, layer_step(): jnp.dot(first_hop[direction].reshape(-1, channels), hop_one_mix[0, direct...  19.9 us
  transfers between devices with their start and end apart: 76, of which 62 were waited for; matrix products, arithmetic and copies ran while one was open for 7% of the time, Pallas kernels for 0%

commit v1 on v0

v1 whole, which is shorter than its diff:
```python
import jax
import jax.numpy as jnp
from jax import lax
from jax.sharding import PartitionSpec as P

F32 = jnp.float32
BF16 = jnp.bfloat16


def moved(value, steps):
    count = lax.axis_size("node")
    first, last = (max(0, -steps), min(count, count - steps))
    return lax.ppermute(value, "node", [(source, source + steps) for source in range(first, last)])


def body(
    features_in,
    filter_gate,
    self_mix,
    hop_one_mix,
    hop_two_mix,
    skip_weight,
    tile_values,
    tile_columns,
    tile_counts,
):
    micro, rows, steps_len, channels = features_in.shape
    width = steps_len * channels
    section_index = lax.axis_index("section")
    block_index = lax.axis_index("node")

    conv_all = lax.all_gather(filter_gate.reshape(1, 2 * channels, -1), "section", tiled=True)
    mixes = jnp.concatenate(
        [self_mix[:, None], hop_one_mix, hop_two_mix, skip_weight[:, None]], axis=1
    ).reshape(1, 6 * channels, -1)
    mix_all = lax.all_gather(mixes, "section", tiled=True)

    slot_ids = jnp.arange(tile_values.shape[2], dtype=jnp.int32)
    live = slot_ids[None, :] < tile_counts[:, 0][:, None]
    place = tile_columns[:, 0] - block_index + 1
    onehot = ((place[:, None, :] == jnp.arange(3)[None, :, None]) & live[:, None, :]).astype(BF16)
    near = jnp.einsum("dks,dsij->dikj", onehot, tile_values[:, 0]).astype(BF16)
    near = near.reshape(2, rows, 3 * rows)
    below, above = moved(near, 1), moved(near, -1)
    pad = lambda value, low, high: jnp.pad(value, ((0, 0), (0, 0), (low * rows, high * rows)))
    stacked = jnp.concatenate([pad(below, 0, 2), pad(near, 1, 1), pad(above, 2, 0)], axis=1)
    squared = jnp.einsum("dij,djk->dik", near, stacked, preferred_element_type=F32).astype(BF16)
    hops = jnp.concatenate([pad(near, 1, 1), squared], axis=0).reshape(4 * rows, 5 * rows)

    state = lax.dynamic_index_in_dim(features_in, section_index, 0, keepdims=False)
    state = state.transpose(1, 0, 2)
    layers = conv_all.shape[0]
    total = jnp.zeros((steps_len * rows, channels), F32)
    for layer in range(layers):
        back = 1 + layer % 2
        earlier = jnp.pad(state, ((back, 0), (0, 0), (0, 0)))[:steps_len]
        both = jnp.concatenate([earlier, state], axis=2).reshape(-1, 2 * channels)
        pre_act = jnp.dot(both, conv_all[layer], preferred_element_type=F32)
        hidden = (jnp.tanh(pre_act[:, :channels]) * jax.nn.sigmoid(pre_act[:, channels:])).astype(BF16)
        total = total + jnp.dot(hidden, mix_all[layer, 5 * channels :], preferred_element_type=F32)
        if layer == layers - 1:
            break
        fields = hidden.reshape(steps_len, rows, channels)
        window = jnp.concatenate(
            [moved(fields, 2), moved(fields, 1), fields, moved(fields, -1), moved(fields, -2)], axis=1
        )
        hopped = jnp.einsum("ij,tjc->tic", hops, window, preferred_element_type=F32).astype(BF16)
        hopped = hopped.reshape(steps_len, 4, rows, channels)
        mix = mix_all[layer]
        mixed = jnp.dot(hidden, mix[:channels], preferred_element_type=F32)
        for k in range(4):
            mixed = mixed + jnp.dot(
                hopped[:, k].reshape(-1, channels),
                mix[(1 + k) * channels : (2 + k) * channels],
                preferred_element_type=F32,
            )
        state = (state.astype(F32) + mixed.reshape(state.shape)).astype(BF16)
    out = total.reshape(steps_len, rows, channels).transpose(1, 0, 2)
    parts = lax.all_to_all(
        out.reshape(lax.axis_size("section"), -1, steps_len, channels), "section", 0, 0, tiled=True
    )
    return parts[:, None]


def solution(mesh):
    in_specs = (
        P(None, "node", None, None),
        P("section", None, None, None),
        P("section", None, None),
        P("section", None, None, None),
        P("section", None, None, None),
        P("section", None, None),
        P(None, "node", None, None, None),
        P(None, "node", None),
        P(None, "node"),
    )
    out_specs = P(None, "node", "section", None, None)
    return jax.shard_map(body, mesh=mesh, in_specs=in_specs, out_specs=out_specs, check_vma=False)
```

time: 741 us -> 315 us (0.43)
  waiting for transfers between devices: 277 us -> 76 us
  starting transfers between devices: 243 us -> 103 us
  local copies, waits for them, and re-layouts: 71.7 us -> 25.7 us
  matrix products: 95.8 us -> 65.7 us
  other arithmetic: 27.8 us -> 6.3 us
  blocking collectives: 0 us -> 17.5 us
    ppermute x75 -> x30, waiting for transfers between devices: 232 us -> 31.1 us  [moved(): lax.ppermute(value, 'node', [(source, source + steps) for source in range...]
    ppermute x75 -> x30, starting transfers between devices: 243 us -> 103 us  [moved(): lax.ppermute(value, 'node', [(source, source + steps) for source in range...]
    reduce_scatter x1 -> x0, waiting for transfers between devices: 44.9 us -> none  [body(): lax.psum_scatter(skip_acc.reshape(micro, 1, tile_rows, steps_len, skip_wi...]
    all_gather x0 -> x2, waiting for transfers between devices: none -> 44.1 us  [the longest x1 25.6 us: body(): lax.all_gather(filter_gate.reshape(1, 2 * channels, -1), 'section', tiled...]
    dynamic_slice x30 -> x0, local copies, waits for them, and re-layouts: 30.6 us -> none  [the longest x15 15.4 us: tick_body(): lax.dynamic_index_in_dim(skip_acc, sample_slot, 0, keepdims=False)]
    dot_general x151 -> x60, matrix products: 95.8 us -> 65.7 us  [the longest x28 31.5 us: body(): jnp.dot(hopped[:, k].reshape(-1, channels), mix[(1 + k) * channels:(2 + k...]
    select_n x30 -> x0, other arithmetic: 21.8 us -> none  [the longest x15 17.6 us: tick_body(): current = jnp.where(section_index == 0, fresh, state)]
    all_to_all x0 -> x1, blocking collectives: none -> 17.5 us  [body(): lax.all_to_all(out.reshape(lax.axis_size('section'), -1, steps_len, chann...]
  transfers between devices with their start and end apart: 76 -> 32, of which waited for: 62 -> 11; matrix products, arithmetic and copies ran while one was open for 7% -> 9% of each run, Pallas kernels for 0% -> 0%
where the time goes in v1:
time: 315 us; the launch traced here: 310 us
  starting transfers between devices  103 us (33%)
  waiting for transfers between devices  76 us (24%)
  matrix products  65.7 us (21%)
  local copies, waits for them, and re-layouts  25.7 us (8%)
  blocking collectives  17.5 us (6%)
  between operations  15.1 us (5%)
  other arithmetic  6.3 us (2%)
    ppermute x30, starting transfers between devices, moved(): lax.ppermute(value, 'node', [(source, source + steps) for source in range...  103 us
    dot_general x28, matrix products, body(): jnp.dot(hopped[:, k].reshape(-1, channels), mix[(1 + k) * channels:(2 + k...  31.5 us
    ppermute x30, waiting for transfers between devices, moved(): lax.ppermute(value, 'node', [(source, source + steps) for source in range...  31.1 us
    all_gather x1, waiting for transfers between devices, body(): lax.all_gather(filter_gate.reshape(1, 2 * channels, -1), 'section', tiled...  25.6 us
    all_gather x1, waiting for transfers between devices, body(): mix_all = lax.all_gather(mixes, 'section', tiled=True)  18.5 us
    all_to_all x1, blocking collectives, body(): lax.all_to_all(out.reshape(lax.axis_size('section'), -1, steps_len, chann...  17.5 us
    unnamed x73, local copies, waits for them, and re-layouts  12 us
    dot_general x8, matrix products, body(): pre_act = jnp.dot(both, conv_all[layer], preferred_element_type=F32)  11.2 us
  transfers between devices with their start and end apart: 32, of which 11 were waited for; matrix products, arithmetic and copies ran while one was open for 9% of the time, Pallas kernels for 0%

profile of v1, /device:TPU:121, one launch (start us, length us, event | category | flops | bytes accessed | tf_op | source)
XLA Modules:
  0.0 309.8 jit_solution(17130637104213180096)
XLA Ops:
  7.3 2.1 pad_maximum_fusion
  11.5 3.9 %collective-permute-start.5 = (bf16[2,128,384]{2,1,0:T(8,128)(2,1)S(1)}, bf16[2,128,384]{2,1,0:T(8,128)(2,1)S(1)}, u32[]{:S(2)}, u32[]{:S(2)}) collective-permute-start(bf16[2,128,384]{2,1,0:T(8,128)(2,1)S(1)} %copy.123), channel_id=1, source_target_pairs={{1,0},{2,1},{3,2},{4,3},{5,4},{6,5},{7,6},{8,7},{9,8},{10,9},{11,1... | collective-permute-start | bytes 589832 | tf_op jit(solution)/shard_map/ppermute | solution.py:13
  15.5 1.9 collective-permute-start.4
  18.4 25.6 %all-gather.3.cloned.1.call-done = bf16[8,512,512]{2,1,0:T(8,128)(2,1)} async-done(((bf16[1,512,512]{2,1,0:T(8,128)(2,1)}), bf16[8,512,512]{2,1,0:T(8,128)(2,1)}) %all-gather.3.cloned.1.call-update) | async-done | bytes 4194320 | tf_op jit(solution)/shard_map/all_gather | solution.py:32
  44.1 1.4 fusion.25
  45.8 4.6 %collective-permute-start = (bf16[3,128,256]{1,2,0:T(8,128)(2,1)S(1)}, bf16[3,128,256]{1,2,0:T(8,128)(2,1)S(1)}, u32[]{:S(2)}, u32[]{:S(2)}) collective-permute-start(bf16[3,128,256]{1,2,0:T(8,128)(2,1)S(1)} %copy.116), channel_id=1, source_target_pairs={{0,2},{1,3},{2,4},{3,5},{4,6},{5,7},{6,8},{7,9},{8,10},{9,11},{10,... | collective-permute-start | bytes 589832 | tf_op jit(solution)/shard_map/ppermute | solution.py:13
  50.8 2.2 collective-permute-start.1
  53.1 5.2 %collective-permute-start.2 = (bf16[3,128,256]{1,2,0:T(8,128)(2,1)S(1)}, bf16[3,128,256]{1,2,0:T(8,128)(2,1)S(1)}, u32[]{:S(2)}, u32[]{:S(2)}) collective-permute-start(bf16[3,128,256]{1,2,0:T(8,128)(2,1)S(1)} %copy.116), channel_id=1, source_target_pairs={{1,0},{2,1},{3,2},{4,3},{5,4},{6,5},{7,6},{8,7},{9,8},{10,9},{11,1... | collective-permute-start | bytes 589832 | tf_op jit(solution)/shard_map/ppermute | solution.py:13
  58.3 1.9 collective-permute-start.3
  61.8 5.3 %collective-permute-done.3 = bf16[3,128,256]{1,2,0:T(8,128)(2,1)S(1)} collective-permute-done((bf16[3,128,256]{1,2,0:T(8,128)(2,1)S(1)}, bf16[3,128,256]{1,2,0:T(8,128)(2,1)S(1)}, u32[]{:S(2)}, u32[]{:S(2)}) %collective-permute-start.3) | collective-permute-done | bytes 196640 | tf_op jit(solution)/shard_map/ppermute | solution.py:13
  68.1 1.4 fusion.94
  70.9 18.5 %all-gather.5.cloned.1.call-done = bf16[8,1536,256]{2,1,0:T(8,128)(2,1)} async-done(((bf16[1,1536,256]{2,1,0:T(8,128)(2,1)}), bf16[8,1536,256]{2,1,0:T(8,128)(2,1)}) %all-gather.5.cloned.1.call-update) | async-done | bytes 6291472 | tf_op jit(solution)/shard_map/all_gather | solution.py:36
  96.0 1.4 fusion.24
  97.8 4.6 %collective-permute-start.6 = (bf16[3,128,256]{1,2,0:T(8,128)(2,1)S(1)}, bf16[3,128,256]{1,2,0:T(8,128)(2,1)S(1)}, u32[]{:S(2)}, u32[]{:S(2)}) collective-permute-start(bf16[3,128,256]{1,2,0:T(8,128)(2,1)S(1)} %copy.131), channel_id=1, source_target_pairs={{0,2},{1,3},{2,4},{3,5},{4,6},{5,7},{6,8},{7,9},{8,10},{9,11},{10,... | collective-permute-start | bytes 589832 | tf_op jit(solution)/shard_map/ppermute | solution.py:13
  102.4 2.2 collective-permute-start.7
  104.6 5.2 %collective-permute-start.8 = (bf16[3,128,256]{1,2,0:T(8,128)(2,1)S(1)}, bf16[3,128,256]{1,2,0:T(8,128)(2,1)S(1)}, u32[]{:S(2)}, u32[]{:S(2)}) collective-permute-start(bf16[3,128,256]{1,2,0:T(8,128)(2,1)S(1)} %copy.131), channel_id=1, source_target_pairs={{1,0},{2,1},{3,2},{4,3},{5,4},{6,5},{7,6},{8,7},{9,8},{10,9},{11,1... | collective-permute-start | bytes 589832 | tf_op jit(solution)/shard_map/ppermute | solution.py:13
  109.8 1.9 collective-permute-start.9
  112.8 1.1 convolution_add_fusion.30
  115.3 3.2 %collective-permute-done.9 = bf16[3,128,256]{1,2,0:T(8,128)(2,1)S(1)} collective-permute-done((bf16[3,128,256]{1,2,0:T(8,128)(2,1)S(1)}, bf16[3,128,256]{1,2,0:T(8,128)(2,1)S(1)}, u32[]{:S(2)}, u32[]{:S(2)}) %collective-permute-start.9) | collective-permute-done | bytes 196640 | tf_op jit(solution)/shard_map/ppermute | solution.py:13
  119.5 1.4 fusion.93
  123.5 1.2 convolution_add_fusion.28
  127.0 1.4 fusion.23
  128.8 7.9 %collective-permute-start.10 = (bf16[3,128,256]{1,2,0:T(8,128)(2,1)S(1)}, bf16[3,128,256]{1,2,0:T(8,128)(2,1)S(1)}, u32[]{:S(2)}, u32[]{:S(2)}) collective-permute-start(bf16[3,128,256]{1,2,0:T(8,128)(2,1)S(1)} %copy.140), channel_id=1, source_target_pairs={{0,2},{1,3},{2,4},{3,5},{4,6},{5,7},{6,8},{7,9},{8,10},{9,11},{10,... | collective-permute-start | bytes 589832 | tf_op jit(solution)/shard_map/ppermute | solution.py:13
  136.7 1.9 collective-permute-start.11
  138.6 5.5 %collective-permute-start.12 = (bf16[3,128,256]{1,2,0:T(8,128)(2,1)S(1)}, bf16[3,128,256]{1,2,0:T(8,128)(2,1)S(1)}, u32[]{:S(2)}, u32[]{:S(2)}) collective-permute-start(bf16[3,128,256]{1,2,0:T(8,128)(2,1)S(1)} %copy.140), channel_id=1, source_target_pairs={{1,0},{2,1},{3,2},{4,3},{5,4},{6,5},{7,6},{8,7},{9,8},{10,9},{11,1... | collective-permute-start | bytes 589832 | tf_op jit(solution)/shard_map/ppermute | solution.py:13
  144.1 2.1 collective-permute-start.13
  148.7 3.3 %collective-permute-done.13 = bf16[3,128,256]{1,2,0:T(8,128)(2,1)S(1)} collective-permute-done((bf16[3,128,256]{1,2,0:T(8,128)(2,1)S(1)}, bf16[3,128,256]{1,2,0:T(8,128)(2,1)S(1)}, u32[]{:S(2)}, u32[]{:S(2)}) %collective-permute-start.13) | collective-permute-done | bytes 196640 | tf_op jit(solution)/shard_map/ppermute | solution.py:13
  153.1 1.4 fusion.92
  157.0 1.2 convolution_add_fusion.23
  160.6 1.4 fusion.22
  162.3 3.9 %collective-permute-start.14 = (bf16[3,128,256]{1,2,0:T(8,128)(2,1)S(1)}, bf16[3,128,256]{1,2,0:T(8,128)(2,1)S(1)}, u32[]{:S(2)}, u32[]{:S(2)}) collective-permute-start(bf16[3,128,256]{1,2,0:T(8,128)(2,1)S(1)} %copy.149), channel_id=1, source_target_pairs={{0,2},{1,3},{2,4},{3,5},{4,6},{5,7},{6,8},{7,9},{8,10},{9,11},{10,... | collective-permute-start | bytes 589832 | tf_op jit(solution)/shard_map/ppermute | solution.py:13
  166.2 1.9 collective-permute-start.15
  168.1 5.5 %collective-permute-start.16 = (bf16[3,128,256]{1,2,0:T(8,128)(2,1)S(1)}, bf16[3,128,256]{1,2,0:T(8,128)(2,1)S(1)}, u32[]{:S(2)}, u32[]{:S(2)}) collective-permute-start(bf16[3,128,256]{1,2,0:T(8,128)(2,1)S(1)} %copy.149), channel_id=1, source_target_pairs={{1,0},{2,1},{3,2},{4,3},{5,4},{6,5},{7,6},{8,7},{9,8},{10,9},{11,1... | collective-permute-start | bytes 589832 | tf_op jit(solution)/shard_map/ppermute | solution.py:13
  173.6 1.9 collective-permute-start.17
  178.0 3.5 %collective-permute-done.17 = bf16[3,128,256]{1,2,0:T(8,128)(2,1)S(1)} collective-permute-done((bf16[3,128,256]{1,2,0:T(8,128)(2,1)S(1)}, bf16[3,128,256]{1,2,0:T(8,128)(2,1)S(1)}, u32[]{:S(2)}, u32[]{:S(2)}) %collective-permute-start.17) | collective-permute-done | bytes 196640 | tf_op jit(solution)/shard_map/ppermute | solution.py:13
  182.6 1.4 fusion.91
  186.5 1.2 convolution_add_fusion.18
  190.1 1.4 fusion.21
  191.8 3.4 %collective-permute-start.18 = (bf16[3,128,256]{1,2,0:T(8,128)(2,1)S(1)}, bf16[3,128,256]{1,2,0:T(8,128)(2,1)S(1)}, u32[]{:S(2)}, u32[]{:S(2)}) collective-permute-start(bf16[3,128,256]{1,2,0:T(8,128)(2,1)S(1)} %copy.158), channel_id=1, source_target_pairs={{0,2},{1,3},{2,4},{3,5},{4,6},{5,7},{6,8},{7,9},{8,10},{9,11},{10,... | collective-permute-start | bytes 589832 | tf_op jit(solution)/shard_map/ppermute | solution.py:13
  195.2 1.9 collective-permute-start.19
  197.2 5.5 %collective-permute-start.20 = (bf16[3,128,256]{1,2,0:T(8,128)(2,1)S(1)}, bf16[3,128,256]{1,2,0:T(8,128)(2,1)S(1)}, u32[]{:S(2)}, u32[]{:S(2)}) collective-permute-start(bf16[3,128,256]{1,2,0:T(8,128)(2,1)S(1)} %copy.158), channel_id=1, source_target_pairs={{1,0},{2,1},{3,2},{4,3},{5,4},{6,5},{7,6},{8,7},{9,8},{10,9},{11,1... | collective-permute-start | bytes 589832 | tf_op jit(solution)/shard_map/ppermute | solution.py:13
  202.6 2.1 collective-permute-start.21
  207.3 4.6 %collective-permute-done.21 = bf16[3,128,256]{1,2,0:T(8,128)(2,1)S(1)} collective-permute-done((bf16[3,128,256]{1,2,0:T(8,128)(2,1)S(1)}, bf16[3,128,256]{1,2,0:T(8,128)(2,1)S(1)}, u32[]{:S(2)}, u32[]{:S(2)}) %collective-permute-start.21) | collective-permute-done | bytes 196640 | tf_op jit(solution)/shard_map/ppermute | solution.py:13
  212.9 1.4 fusion.90
  216.9 1.2 convolution_add_fusion.13
  220.4 1.4 fusion.20
  222.1 2.4 collective-permute-start.22
  224.5 1.9 collective-permute-start.23
  226.4 5.5 %collective-permute-start.24 = (bf16[3,128,256]{1,2,0:T(8,128)(2,1)S(1)}, bf16[3,128,256]{1,2,0:T(8,128)(2,1)S(1)}, u32[]{:S(2)}, u32[]{:S(2)}) collective-permute-start(bf16[3,128,256]{1,2,0:T(8,128)(2,1)S(1)} %copy.167), channel_id=1, source_target_pairs={{1,0},{2,1},{3,2},{4,3},{5,4},{6,5},{7,6},{8,7},{9,8},{10,9},{11,1... | collective-permute-start | bytes 589832 | tf_op jit(solution)/shard_map/ppermute | solution.py:13
  231.9 3.4 %collective-permute-start.25 = (bf16[3,128,256]{1,2,0:T(8,128)(2,1)S(1)}, bf16[3,128,256]{1,2,0:T(8,128)(2,1)S(1)}, u32[]{:S(2)}, u32[]{:S(2)}) collective-permute-start(bf16[3,128,256]{1,2,0:T(8,128)(2,1)S(1)} %copy.167), channel_id=1, source_target_pairs={{2,0},{3,1},{4,2},{5,3},{6,4},{7,5},{8,6},{9,7},{10,8},{11,9},{12,... | collective-permute-start | bytes 589832 | tf_op jit(solution)/shard_map/ppermute | solution.py:13
  237.8 4.9 %collective-permute-done.25 = bf16[3,128,256]{1,2,0:T(8,128)(2,1)S(1)} collective-permute-done((bf16[3,128,256]{1,2,0:T(8,128)(2,1)S(1)}, bf16[3,128,256]{1,2,0:T(8,128)(2,1)S(1)}, u32[]{:S(2)}, u32[]{:S(2)}) %collective-permute-start.25) | collective-permute-done | bytes 196640 | tf_op jit(solution)/shard_map/ppermute | solution.py:13
  243.7 1.4 fusion.89
  247.7 1.2 convolution_add_fusion.8
  251.2 1.4 fusion.19
  253.0 2.1 collective-permute-start.26
  255.1 1.9 collective-permute-start.27
  257.0 5.5 %collective-permute-start.28 = (bf16[3,128,256]{1,2,0:T(8,128)(2,1)S(1)}, bf16[3,128,256]{1,2,0:T(8,128)(2,1)S(1)}, u32[]{:S(2)}, u32[]{:S(2)}) collective-permute-start(bf16[3,128,256]{1,2,0:T(8,128)(2,1)S(1)} %copy.176), channel_id=1, source_target_pairs={{1,0},{2,1},{3,2},{4,3},{5,4},{6,5},{7,6},{8,7},{9,8},{10,9},{11,1... | collective-permute-start | bytes 589832 | tf_op jit(solution)/shard_map/ppermute | solution.py:13
  262.5 3.5 %collective-permute-start.29 = (bf16[3,128,256]{1,2,0:T(8,128)(2,1)S(1)}, bf16[3,128,256]{1,2,0:T(8,128)(2,1)S(1)}, u32[]{:S(2)}, u32[]{:S(2)}) collective-permute-start(bf16[3,128,256]{1,2,0:T(8,128)(2,1)S(1)} %copy.176), channel_id=1, source_target_pairs={{2,0},{3,1},{4,2},{5,3},{6,4},{7,5},{8,6},{9,7},{10,8},{11,9},{12,... | collective-permute-start | bytes 589832 | tf_op jit(solution)/shard_map/ppermute | solution.py:13
  268.4 5.1 %collective-permute-done.29 = bf16[3,128,256]{1,2,0:T(8,128)(2,1)S(1)} collective-permute-done((bf16[3,128,256]{1,2,0:T(8,128)(2,1)S(1)}, bf16[3,128,256]{1,2,0:T(8,128)(2,1)S(1)}, u32[]{:S(2)}, u32[]{:S(2)}) %collective-permute-start.29) | collective-permute-done | bytes 196640 | tf_op jit(solution)/shard_map/ppermute | solution.py:13
  274.5 1.4 fusion.88
  277.4 1.1 convolution_add_fusion.4
  282.0 1.4 fusion.18
  283.4 1.2 convolution_add_fusion
  284.6 17.5 %all_to_all.5 = f32[8,16,3,256]{3,1,2,0:T(8,128)S(1)} all-to-all(f32[8,16,3,256]{3,1,2,0:T(8,128)S(1)} %copy.185), channel_id=1, replica_groups=mesh['section'=8,'node'=32] {'section'}, dimensions={0} | all-to-all | bytes 786432 | tf_op jit(solution)/shard_map/all_to_all | solution.py:79
  (203 shorter events, 67.6 us)
Async XLA Ops:
  6.5 4.3 %copy-start = (bf16[2,1,3,128,128]{4,3,2,1,0:T(8,128)(2,1)S(1)}, bf16[2,1,3,128,128]{4,3,2,1,0:T(8,128)(2,1)}, u32[]{:S(2)}) copy-start(bf16[2,1,3,128,128]{4,3,2,1,0:T(8,128)(2,1)} %param.15) | copy-start | bytes 589828
  6.5 37.5 %all-gather.3.cloned.1.call-start = ((), (), s32[]{:S(2)}) async-start(), calls=%async_computation.1 | async-start | bytes 4718592 | tf_op jit(solution)/shard_map/all_gather | solution.py:32
  7.3 82.1 %all-gather.5.cloned.1.call-start = ((), (), s32[]{:S(2)}) async-start(), calls=%async_computation.2 | async-start | bytes 7077888 | tf_op jit(solution)/shard_map/all_gather | solution.py:36
  11.5 38.9 %collective-permute-start.5 = (bf16[2,128,384]{2,1,0:T(8,128)(2,1)S(1)}, bf16[2,128,384]{2,1,0:T(8,128)(2,1)S(1)}, u32[]{:S(2)}, u32[]{:S(2)}) collective-permute-start(bf16[2,128,384]{2,1,0:T(8,128)(2,1)S(1)} %copy.123), channel_id=1, source_target_pairs={{1,0},{2,1},{3,2},{4,3},{5,4},{6,5},{7,6},{8,7},{9,8},{10,9},{11,1... | collective-permute-start | bytes 589832 | tf_op jit(solution)/shard_map/ppermute | solution.py:13
  15.5 35.0 %collective-permute-start.4 = (bf16[2,128,384]{2,1,0:T(8,128)(2,1)S(1)}, bf16[2,128,384]{2,1,0:T(8,128)(2,1)S(1)}, u32[]{:S(2)}, u32[]{:S(2)}) collective-permute-start(bf16[2,128,384]{2,1,0:T(8,128)(2,1)S(1)} %copy.123), channel_id=1, source_target_pairs={{0,1},{1,2},{2,3},{3,4},{4,5},{5,6},{6,7},{7,8},{8,9},{9,10},{10,1... | collective-permute-start | bytes 589832 | tf_op jit(solution)/shard_map/ppermute | solution.py:13
  45.8 14.5 %collective-permute-start = (bf16[3,128,256]{1,2,0:T(8,128)(2,1)S(1)}, bf16[3,128,256]{1,2,0:T(8,128)(2,1)S(1)}, u32[]{:S(2)}, u32[]{:S(2)}) collective-permute-start(bf16[3,128,256]{1,2,0:T(8,128)(2,1)S(1)} %copy.116), channel_id=1, source_target_pairs={{0,2},{1,3},{2,4},{3,5},{4,6},{5,7},{6,8},{7,9},{8,10},{9,11},{10,... | collective-permute-start | bytes 589832 | tf_op jit(solution)/shard_map/ppermute | solution.py:13
  50.8 10.1 %collective-permute-start.1 = (bf16[3,128,256]{1,2,0:T(8,128)(2,1)S(1)}, bf16[3,128,256]{1,2,0:T(8,128)(2,1)S(1)}, u32[]{:S(2)}, u32[]{:S(2)}) collective-permute-start(bf16[3,128,256]{1,2,0:T(8,128)(2,1)S(1)} %copy.116), channel_id=1, source_target_pairs={{0,1},{1,2},{2,3},{3,4},{4,5},{5,6},{6,7},{7,8},{8,9},{9,10},{10,1... | collective-permute-start | bytes 589832 | tf_op jit(solution)/shard_map/ppermute | solution.py:13
  53.1 65.4 %copy-start.2 = (bf16[4,128,640]{2,1,0:T(8,128)(2,1)}, bf16[4,128,640]{2,1,0:T(8,128)(2,1)S(1)}, u32[]{:S(2)}) copy-start(bf16[4,128,640]{2,1,0:T(8,128)(2,1)S(1)} %pad_maximum_fusion.1) | copy-start | bytes 1966084
  53.1 8.6 %collective-permute-start.2 = (bf16[3,128,256]{1,2,0:T(8,128)(2,1)S(1)}, bf16[3,128,256]{1,2,0:T(8,128)(2,1)S(1)}, u32[]{:S(2)}, u32[]{:S(2)}) collective-permute-start(bf16[3,128,256]{1,2,0:T(8,128)(2,1)S(1)} %copy.116), channel_id=1, source_target_pairs={{1,0},{2,1},{3,2},{4,3},{5,4},{6,5},{7,6},{8,7},{9,8},{10,9},{11,1... | collective-permute-start | bytes 589832 | tf_op jit(solution)/shard_map/ppermute | solution.py:13
  58.3 8.7 %collective-permute-start.3 = (bf16[3,128,256]{1,2,0:T(8,128)(2,1)S(1)}, bf16[3,128,256]{1,2,0:T(8,128)(2,1)S(1)}, u32[]{:S(2)}, u32[]{:S(2)}) collective-permute-start(bf16[3,128,256]{1,2,0:T(8,128)(2,1)S(1)} %copy.116), channel_id=1, source_target_pairs={{2,0},{3,1},{4,2},{5,3},{6,4},{7,5},{8,6},{9,7},{10,8},{11,9},{12,... | collective-permute-start | bytes 589832 | tf_op jit(solution)/shard_map/ppermute | solution.py:13
  97.8 17.3 %collective-permute-start.6 = (bf16[3,128,256]{1,2,0:T(8,128)(2,1)S(1)}, bf16[3,128,256]{1,2,0:T(8,128)(2,1)S(1)}, u32[]{:S(2)}, u32[]{:S(2)}) collective-permute-start(bf16[3,128,256]{1,2,0:T(8,128)(2,1)S(1)} %copy.131), channel_id=1, source_target_pairs={{0,2},{1,3},{2,4},{3,5},{4,6},{5,7},{6,8},{7,9},{8,10},{9,11},{10,... | collective-permute-start | bytes 589832 | tf_op jit(solution)/shard_map/ppermute | solution.py:13
  102.4 12.7 %collective-permute-start.7 = (bf16[3,128,256]{1,2,0:T(8,128)(2,1)S(1)}, bf16[3,128,256]{1,2,0:T(8,128)(2,1)S(1)}, u32[]{:S(2)}, u32[]{:S(2)}) collective-permute-start(bf16[3,128,256]{1,2,0:T(8,128)(2,1)S(1)} %copy.131), channel_id=1, source_target_pairs={{0,1},{1,2},{2,3},{3,4},{4,5},{5,6},{6,7},{7,8},{8,9},{9,10},{10,1... | collective-permute-start | bytes 589832 | tf_op jit(solution)/shard_map/ppermute | solution.py:13
  104.6 10.7 %collective-permute-start.8 = (bf16[3,128,256]{1,2,0:T(8,128)(2,1)S(1)}, bf16[3,128,256]{1,2,0:T(8,128)(2,1)S(1)}, u32[]{:S(2)}, u32[]{:S(2)}) collective-permute-start(bf16[3,128,256]{1,2,0:T(8,128)(2,1)S(1)} %copy.131), channel_id=1, source_target_pairs={{1,0},{2,1},{3,2},{4,3},{5,4},{6,5},{7,6},{8,7},{9,8},{10,9},{11,1... | collective-permute-start | bytes 589832 | tf_op jit(solution)/shard_map/ppermute | solution.py:13
  109.8 8.7 %collective-permute-start.9 = (bf16[3,128,256]{1,2,0:T(8,128)(2,1)S(1)}, bf16[3,128,256]{1,2,0:T(8,128)(2,1)S(1)}, u32[]{:S(2)}, u32[]{:S(2)}) collective-permute-start(bf16[3,128,256]{1,2,0:T(8,128)(2,1)S(1)} %copy.131), channel_id=1, source_target_pairs={{2,0},{3,1},{4,2},{5,3},{6,4},{7,5},{8,6},{9,7},{10,8},{11,9},{12,... | collective-permute-start | bytes 589832 | tf_op jit(solution)/shard_map/ppermute | solution.py:13
  123.5 28.6 %copy-start.3 = (bf16[4,128,640]{2,1,0:T(8,128)(2,1)S(1)}, bf16[4,128,640]{2,1,0:T(8,128)(2,1)}, u32[]{:S(2)}) copy-start(bf16[4,128,640]{2,1,0:T(8,128)(2,1)} %copy-done.2) | copy-start | bytes 1966084
  128.8 19.7 %collective-permute-start.10 = (bf16[3,128,256]{1,2,0:T(8,128)(2,1)S(1)}, bf16[3,128,256]{1,2,0:T(8,128)(2,1)S(1)}, u32[]{:S(2)}, u32[]{:S(2)}) collective-permute-start(bf16[3,128,256]{1,2,0:T(8,128)(2,1)S(1)} %copy.140), channel_id=1, source_target_pairs={{0,2},{1,3},{2,4},{3,5},{4,6},{5,7},{6,8},{7,9},{8,10},{9,11},{10,... | collective-permute-start | bytes 589832 | tf_op jit(solution)/shard_map/ppermute | solution.py:13
  136.7 11.8 %collective-permute-start.11 = (bf16[3,128,256]{1,2,0:T(8,128)(2,1)S(1)}, bf16[3,128,256]{1,2,0:T(8,128)(2,1)S(1)}, u32[]{:S(2)}, u32[]{:S(2)}) collective-permute-start(bf16[3,128,256]{1,2,0:T(8,128)(2,1)S(1)} %copy.140), channel_id=1, source_target_pairs={{0,1},{1,2},{2,3},{3,4},{4,5},{5,6},{6,7},{7,8},{8,9},{9,10},{10,1... | collective-permute-start | bytes 589832 | tf_op jit(solution)/shard_map/ppermute | solution.py:13
  138.6 10.0 %collective-permute-start.12 = (bf16[3,128,256]{1,2,0:T(8,128)(2,1)S(1)}, bf16[3,128,256]{1,2,0:T(8,128)(2,1)S(1)}, u32[]{:S(2)}, u32[]{:S(2)}) collective-permute-start(bf16[3,128,256]{1,2,0:T(8,128)(2,1)S(1)} %copy.140), channel_id=1, source_target_pairs={{1,0},{2,1},{3,2},{4,3},{5,4},{6,5},{7,6},{8,7},{9,8},{10,9},{11,1... | collective-permute-start | bytes 589832 | tf_op jit(solution)/shard_map/ppermute | solution.py:13
  144.1 7.9 %collective-permute-start.13 = (bf16[3,128,256]{1,2,0:T(8,128)(2,1)S(1)}, bf16[3,128,256]{1,2,0:T(8,128)(2,1)S(1)}, u32[]{:S(2)}, u32[]{:S(2)}) collective-permute-start(bf16[3,128,256]{1,2,0:T(8,128)(2,1)S(1)} %copy.140), channel_id=1, source_target_pairs={{2,0},{3,1},{4,2},{5,3},{6,4},{7,5},{8,6},{9,7},{10,8},{11,9},{12,... | collective-permute-start | bytes 589832 | tf_op jit(solution)/shard_map/ppermute | solution.py:13
  157.0 24.6 %copy-start.4 = (bf16[4,128,640]{2,1,0:T(8,128)(2,1)S(1)}, bf16[4,128,640]{2,1,0:T(8,128)(2,1)}, u32[]{:S(2)}) copy-start(bf16[4,128,640]{2,1,0:T(8,128)(2,1)} %copy-done.2) | copy-start | bytes 1966084
  162.3 15.5 %collective-permute-start.14 = (bf16[3,128,256]{1,2,0:T(8,128)(2,1)S(1)}, bf16[3,128,256]{1,2,0:T(8,128)(2,1)S(1)}, u32[]{:S(2)}, u32[]{:S(2)}) collective-permute-start(bf16[3,128,256]{1,2,0:T(8,128)(2,1)S(1)} %copy.149), channel_id=1, source_target_pairs={{0,2},{1,3},{2,4},{3,5},{4,6},{5,7},{6,8},{7,9},{8,10},{9,11},{10,... | collective-permute-start | bytes 589832 | tf_op jit(solution)/shard_map/ppermute | solution.py:13
  166.2 11.6 %collective-permute-start.15 = (bf16[3,128,256]{1,2,0:T(8,128)(2,1)S(1)}, bf16[3,128,256]{1,2,0:T(8,128)(2,1)S(1)}, u32[]{:S(2)}, u32[]{:S(2)}) collective-permute-start(bf16[3,128,256]{1,2,0:T(8,128)(2,1)S(1)} %copy.149), channel_id=1, source_target_pairs={{0,1},{1,2},{2,3},{3,4},{4,5},{5,6},{6,7},{7,8},{8,9},{9,10},{10,1... | collective-permute-start | bytes 589832 | tf_op jit(solution)/shard_map/ppermute | solution.py:13
  168.1 9.8 %collective-permute-start.16 = (bf16[3,128,256]{1,2,0:T(8,128)(2,1)S(1)}, bf16[3,128,256]{1,2,0:T(8,128)(2,1)S(1)}, u32[]{:S(2)}, u32[]{:S(2)}) collective-permute-start(bf16[3,128,256]{1,2,0:T(8,128)(2,1)S(1)} %copy.149), channel_id=1, source_target_pairs={{1,0},{2,1},{3,2},{4,3},{5,4},{6,5},{7,6},{8,7},{9,8},{10,9},{11,1... | collective-permute-start | bytes 589832 | tf_op jit(solution)/shard_map/ppermute | solution.py:13
  173.6 7.9 %collective-permute-start.17 = (bf16[3,128,256]{1,2,0:T(8,128)(2,1)S(1)}, bf16[3,128,256]{1,2,0:T(8,128)(2,1)S(1)}, u32[]{:S(2)}, u32[]{:S(2)}) collective-permute-start(bf16[3,128,256]{1,2,0:T(8,128)(2,1)S(1)} %copy.149), channel_id=1, source_target_pairs={{2,0},{3,1},{4,2},{5,3},{6,4},{7,5},{8,6},{9,7},{10,8},{11,9},{12,... | collective-permute-start | bytes 589832 | tf_op jit(solution)/shard_map/ppermute | solution.py:13
  186.5 25.4 %copy-start.5 = (bf16[4,128,640]{2,1,0:T(8,128)(2,1)S(1)}, bf16[4,128,640]{2,1,0:T(8,128)(2,1)}, u32[]{:S(2)}) copy-start(bf16[4,128,640]{2,1,0:T(8,128)(2,1)} %copy-done.2) | copy-start | bytes 1966084
  191.8 15.2 %collective-permute-start.18 = (bf16[3,128,256]{1,2,0:T(8,128)(2,1)S(1)}, bf16[3,128,256]{1,2,0:T(8,128)(2,1)S(1)}, u32[]{:S(2)}, u32[]{:S(2)}) collective-permute-start(bf16[3,128,256]{1,2,0:T(8,128)(2,1)S(1)} %copy.158), channel_id=1, source_target_pairs={{0,2},{1,3},{2,4},{3,5},{4,6},{5,7},{6,8},{7,9},{8,10},{9,11},{10,... | collective-permute-start | bytes 589832 | tf_op jit(solution)/shard_map/ppermute | solution.py:13
  195.2 11.8 %collective-permute-start.19 = (bf16[3,128,256]{1,2,0:T(8,128)(2,1)S(1)}, bf16[3,128,256]{1,2,0:T(8,128)(2,1)S(1)}, u32[]{:S(2)}, u32[]{:S(2)}) collective-permute-start(bf16[3,128,256]{1,2,0:T(8,128)(2,1)S(1)} %copy.158), channel_id=1, source_target_pairs={{0,1},{1,2},{2,3},{3,4},{4,5},{5,6},{6,7},{7,8},{8,9},{9,10},{10,1... | collective-permute-start | bytes 589832 | tf_op jit(solution)/shard_map/ppermute | solution.py:13
  197.2 10.0 %collective-permute-start.20 = (bf16[3,128,256]{1,2,0:T(8,128)(2,1)S(1)}, bf16[3,128,256]{1,2,0:T(8,128)(2,1)S(1)}, u32[]{:S(2)}, u32[]{:S(2)}) collective-permute-start(bf16[3,128,256]{1,2,0:T(8,128)(2,1)S(1)} %copy.158), channel_id=1, source_target_pairs={{1,0},{2,1},{3,2},{4,3},{5,4},{6,5},{7,6},{8,7},{9,8},{10,9},{11,1... | collective-permute-start | bytes 589832 | tf_op jit(solution)/shard_map/ppermute | solution.py:13
  202.6 9.2 %collective-permute-start.21 = (bf16[3,128,256]{1,2,0:T(8,128)(2,1)S(1)}, bf16[3,128,256]{1,2,0:T(8,128)(2,1)S(1)}, u32[]{:S(2)}, u32[]{:S(2)}) collective-permute-start(bf16[3,128,256]{1,2,0:T(8,128)(2,1)S(1)} %copy.158), channel_id=1, source_target_pairs={{2,0},{3,1},{4,2},{5,3},{6,4},{7,5},{8,6},{9,7},{10,8},{11,9},{12,... | collective-permute-start | bytes 589832 | tf_op jit(solution)/shard_map/ppermute | solution.py:13
  216.9 25.9 %copy-start.6 = (bf16[4,128,640]{2,1,0:T(8,128)(2,1)S(1)}, bf16[4,128,640]{2,1,0:T(8,128)(2,1)}, u32[]{:S(2)}) copy-start(bf16[4,128,640]{2,1,0:T(8,128)(2,1)} %copy-done.2) | copy-start | bytes 1966084
  222.1 15.4 %collective-permute-start.22 = (bf16[3,128,256]{1,2,0:T(8,128)(2,1)S(1)}, bf16[3,128,256]{1,2,0:T(8,128)(2,1)S(1)}, u32[]{:S(2)}, u32[]{:S(2)}) collective-permute-start(bf16[3,128,256]{1,2,0:T(8,128)(2,1)S(1)} %copy.167), channel_id=1, source_target_pairs={{0,2},{1,3},{2,4},{3,5},{4,6},{5,7},{6,8},{7,9},{8,10},{9,11},{10,... | collective-permute-start | bytes 589832 | tf_op jit(solution)/shard_map/ppermute | solution.py:13
  224.5 13.1 %collective-permute-start.23 = (bf16[3,128,256]{1,2,0:T(8,128)(2,1)S(1)}, bf16[3,128,256]{1,2,0:T(8,128)(2,1)S(1)}, u32[]{:S(2)}, u32[]{:S(2)}) collective-permute-start(bf16[3,128,256]{1,2,0:T(8,128)(2,1)S(1)} %copy.167), channel_id=1, source_target_pairs={{0,1},{1,2},{2,3},{3,4},{4,5},{5,6},{6,7},{7,8},{8,9},{9,10},{10,1... | collective-permute-start | bytes 589832 | tf_op jit(solution)/shard_map/ppermute | solution.py:13
  226.4 11.3 %collective-permute-start.24 = (bf16[3,128,256]{1,2,0:T(8,128)(2,1)S(1)}, bf16[3,128,256]{1,2,0:T(8,128)(2,1)S(1)}, u32[]{:S(2)}, u32[]{:S(2)}) collective-permute-start(bf16[3,128,256]{1,2,0:T(8,128)(2,1)S(1)} %copy.167), channel_id=1, source_target_pairs={{1,0},{2,1},{3,2},{4,3},{5,4},{6,5},{7,6},{8,7},{9,8},{10,9},{11,1... | collective-permute-start | bytes 589832 | tf_op jit(solution)/shard_map/ppermute | solution.py:13
  231.9 10.8 %collective-permute-start.25 = (bf16[3,128,256]{1,2,0:T(8,128)(2,1)S(1)}, bf16[3,128,256]{1,2,0:T(8,128)(2,1)S(1)}, u32[]{:S(2)}, u32[]{:S(2)}) collective-permute-start(bf16[3,128,256]{1,2,0:T(8,128)(2,1)S(1)} %copy.167), channel_id=1, source_target_pairs={{2,0},{3,1},{4,2},{5,3},{6,4},{7,5},{8,6},{9,7},{10,8},{11,9},{12,... | collective-permute-start | bytes 589832 | tf_op jit(solution)/shard_map/ppermute | solution.py:13
  247.7 25.9 %copy-start.7 = (bf16[4,128,640]{2,1,0:T(8,128)(2,1)S(1)}, bf16[4,128,640]{2,1,0:T(8,128)(2,1)}, u32[]{:S(2)}) copy-start(bf16[4,128,640]{2,1,0:T(8,128)(2,1)} %copy-done.2) | copy-start | bytes 1966084
  253.0 15.2 %collective-permute-start.26 = (bf16[3,128,256]{1,2,0:T(8,128)(2,1)S(1)}, bf16[3,128,256]{1,2,0:T(8,128)(2,1)S(1)}, u32[]{:S(2)}, u32[]{:S(2)}) collective-permute-start(bf16[3,128,256]{1,2,0:T(8,128)(2,1)S(1)} %copy.176), channel_id=1, source_target_pairs={{0,2},{1,3},{2,4},{3,5},{4,6},{5,7},{6,8},{7,9},{8,10},{9,11},{10,... | collective-permute-start | bytes 589832 | tf_op jit(solution)/shard_map/ppermute | solution.py:13
  255.1 13.2 %collective-permute-start.27 = (bf16[3,128,256]{1,2,0:T(8,128)(2,1)S(1)}, bf16[3,128,256]{1,2,0:T(8,128)(2,1)S(1)}, u32[]{:S(2)}, u32[]{:S(2)}) collective-permute-start(bf16[3,128,256]{1,2,0:T(8,128)(2,1)S(1)} %copy.176), channel_id=1, source_target_pairs={{0,1},{1,2},{2,3},{3,4},{4,5},{5,6},{6,7},{7,8},{8,9},{9,10},{10,1... | collective-permute-start | bytes 589832 | tf_op jit(solution)/shard_map/ppermute | solution.py:13
  257.0 11.4 %collective-permute-start.28 = (bf16[3,128,256]{1,2,0:T(8,128)(2,1)S(1)}, bf16[3,128,256]{1,2,0:T(8,128)(2,1)S(1)}, u32[]{:S(2)}, u32[]{:S(2)}) collective-permute-start(bf16[3,128,256]{1,2,0:T(8,128)(2,1)S(1)} %copy.176), channel_id=1, source_target_pairs={{1,0},{2,1},{3,2},{4,3},{5,4},{6,5},{7,6},{8,7},{9,8},{10,9},{11,1... | collective-permute-start | bytes 589832 | tf_op jit(solution)/shard_map/ppermute | solution.py:13
  262.5 11.0 %collective-permute-start.29 = (bf16[3,128,256]{1,2,0:T(8,128)(2,1)S(1)}, bf16[3,128,256]{1,2,0:T(8,128)(2,1)S(1)}, u32[]{:S(2)}, u32[]{:S(2)}) collective-permute-start(bf16[3,128,256]{1,2,0:T(8,128)(2,1)S(1)} %copy.176), channel_id=1, source_target_pairs={{2,0},{3,1},{4,2},{5,3},{6,4},{7,5},{8,6},{9,7},{10,8},{11,9},{12,... | collective-permute-start | bytes 589832 | tf_op jit(solution)/shard_map/ppermute | solution.py:13
  277.4 25.6 %copy-start.1 = (bf16[2,1,3,128,128]{4,3,2,1,0:T(8,128)(2,1)S(1)}, bf16[2,1,3,128,128]{4,3,2,1,0:T(8,128)(2,1)}, u32[]{:S(2)}) copy-start(bf16[2,1,3,128,128]{4,3,2,1,0:T(8,128)(2,1)} %param.15) | copy-start | bytes 589828
Sparse Core Ops, SparseCore 0:
  9.2 34.7 all-gather.2
  45.9 43.4 all-gather.4

commit v2 on v1

v2 whole, which is shorter than its diff:
```python
import functools

import jax
import jax.numpy as jnp
from jax import lax
from jax.experimental import pallas as pl
from jax.experimental.pallas import tpu as pltpu
from jax.sharding import PartitionSpec as P

F32 = jnp.float32
BF16 = jnp.bfloat16
MESH = pl.DeviceIdType.MESH
XS = 4
YS = 4
LOOK = 6


def both(*conds):
    out = conds[0]
    for cond in conds[1:]:
        out = jnp.logical_and(out, cond)
    return out


def kernel(
    layers,
    blocks,
    feat,
    conv_in,
    self_in,
    one_in,
    two_in,
    skip_in,
    tiles,
    columns,
    counts,
    out,
    xs,
    hb,
    wc,
    wm,
    near,
    rows,
    hops,
    base,
    tot,
    obuf,
    load_sem,
    feat_sem,
    tile_send,
    tile_recv,
    halo_send,
    halo_recv,
    w_send,
    w_recv,
    w_sib,
    out_send,
    out_recv,
):
    steps, tile, ch = feat.shape
    last_layer = layers - 1
    s = lax.axis_index("section")
    n = lax.axis_index("node")
    y, c = lax.div(s, 2), lax.rem(s, 2)
    z, x = lax.div(n, XS), lax.rem(n, XS)
    last = blocks // 2 - 1

    group = lax.rem(lax.div(x + 1, 2), 2)
    side = lax.div(x, 2)
    place = side + lax.rem(z, 2) * (1 - 2 * side)
    k = 2 * z + place
    r = 2 * k + c
    m = 2 * y + group

    def node_at(group, k):
        z, place = lax.div(k, 2), lax.rem(k, 2)
        side = place + lax.rem(z, 2) * (1 - 2 * place)
        return XS * z + group + side * (3 - 2 * group)

    def device(section, node):
        return {"section": section, "node": node}

    def worker(sample, block):
        return device(
            2 * lax.div(sample, 2) + lax.rem(block, 2), node_at(lax.rem(sample, 2), lax.div(block, 2))
        )

    def remote(src, dst, send, recv, dev):
        return pltpu.make_async_remote_copy(
            src_ref=src, dst_ref=dst, send_sem=send, recv_sem=recv, device_id=dev, device_id_type=MESH
        )

    sib = device(2 * y + 1 - c, n)
    right = device(2 * y, node_at(group, jnp.minimum(k + 1, last)))
    left = device(2 * y + 1, node_at(group, jnp.maximum(k - 1, 0)))
    has_right, has_left = k < last, k > 0
    outer_ok = jnp.where(c == 0, has_left, has_right)
    inner_ok = jnp.where(c == 0, has_right, has_left)
    outer_k = jnp.clip(k - 1 + 2 * c, 0, last)
    ring = [lax.rem(y + 1, YS), lax.rem(y + YS - 1, YS)]

    at_home = n == r
    native = both(s == m, at_home)
    mine_to = worker(s, n)
    mine_from = device(m, r)
    n_out = n + 2 * lax.rem(n, 2) - 1
    r_out = r - 1 + 2 * c
    out_slot = 2 * (1 - lax.rem(n, 2))
    out_valid = both(n_out >= 0, n_out < blocks)
    in_valid = both(r_out >= 0, r_out < blocks)
    outer_to = worker(s, jnp.clip(n_out, 0, blocks - 1))
    outer_from = device(m, jnp.clip(r_out, 0, blocks - 1))
    outer_native = both(s == m, n == r_out)

    loads = [
        pltpu.make_async_copy(conv_in, wc.at[s], load_sem.at[0]),
        pltpu.make_async_copy(skip_in, wm.at[s, pl.ds(0, 4)], load_sem.at[1]),
        pltpu.make_async_copy(self_in, wm.at[s, pl.ds(4, 4)], load_sem.at[2]),
        pltpu.make_async_copy(one_in, wm.at[s, pl.ds(8, 8)], load_sem.at[3]),
        pltpu.make_async_copy(two_in, wm.at[s, pl.ds(16, 8)], load_sem.at[4]),
    ]
    for load in loads:
        load.start()

    barrier = pltpu.get_barrier_semaphore()

    def greet(dev):
        pl.semaphore_signal(barrier, inc=1, device_id=dev, device_id_type=MESH)

    greet(sib)
    for near_y in ring:
        for core in range(2):
            greet(device(2 * near_y + core, n))

    @pl.when(outer_ok)
    def _():
        for core in range(2):
            greet(device(2 * y + core, node_at(group, outer_k)))

    @pl.when(jnp.logical_not(native))
    def _():
        greet(mine_from)

    @pl.when(both(in_valid, jnp.logical_not(outer_native)))
    def _():
        greet(outer_from)

    for sample in range(layers):
        @pl.when(jnp.logical_not(both(at_home, m == sample)))
        def _():
            greet(worker(sample, n))

    for e in range(2):
        for w in range(3):
            total = jnp.zeros((tile, tile), F32)
            for slot in range(3):
                weight = both(columns[e, slot] == n - 1 + w, slot < counts[e, 0]).astype(F32)
                total = total + tiles[e, slot].astype(F32) * weight
            near[e, :, w * tile : (w + 1) * tile] = total.astype(BF16)
    xs[0:2] = jnp.zeros((2, tile, ch), BF16)
    tot[...] = jnp.zeros_like(tot)

    @pl.when(jnp.logical_not(outer_ok))
    def _():
        rows[2 * c] = jnp.zeros((2, tile, 3 * tile), BF16)

        @pl.loop(0, last_layer)
        def _(layer):
            for t in range(steps):
                hb[layer, t, 3 * c] = jnp.zeros((tile, ch), BF16)
                hb[layer, t, 3 * c + 1] = jnp.zeros((tile, ch), BF16)

    @pl.when(jnp.logical_not(inner_ok))
    def _():
        @pl.loop(0, last_layer)
        def _(layer):
            for t in range(steps):
                hb[layer, t, 4 - 4 * c] = jnp.zeros((tile, ch), BF16)

    as_int = lambda cond: cond.astype(jnp.int32)
    expected = (
        1
        + 4
        + as_int(has_right)
        + as_int(has_left)
        + 1
        - as_int(native)
        + as_int(both(out_valid, jnp.logical_not(outer_native)))
        + layers
        - as_int(at_home)
    )
    pl.semaphore_wait(barrier, expected)
    for load in loads:
        load.wait()

    def piece(layer, part, first, count):
        if part == 0:
            return wc.at[layer, pl.ds(first, count)]
        return wm.at[layer, pl.ds(12 * (part - 1) + 3 * first, 3 * count)]

    def ring_copy(layer, part, d, core, slot):
        ref = piece(layer, part, 2 * d + core, 1)
        return remote(
            ref, ref, w_send.at[layer, part, d, slot], w_recv.at[layer, part, d], device(2 * ring[d] + core, n)
        )

    def sib_copy(layer, part, d, whole):
        ref = piece(layer, part, 2 * d, 2) if whole else piece(layer, part, 2 * d + c, 1)
        return remote(ref, ref, w_send.at[layer, part, d, 2], w_sib.at[layer, part, d], sib)

    def sib_wait(layer, part, d, whole):
        ref = piece(layer, part, 2 * d, 2) if whole else piece(layer, part, 2 * d + 1 - c, 1)
        remote(ref, ref, w_send.at[layer, part, d, 2], w_sib.at[layer, part, d], sib).wait_recv()

    def distance(layer, d):
        gap = y - lax.div(layer, 2) if d == 0 else lax.div(layer, 2) - y
        return lax.rem(gap + YS, YS)

    def wanted(layer, part):
        valid = both(layer >= 0, layer < layers)
        return both(valid, layer < last_layer) if part == 2 else valid

    def point(l, t):
        for d in range(2):
            for h in range(YS):
                at = t + LOOK - h
                part = at % 3
                layer_at = l + at // 3
                layer = jnp.clip(layer_at, 0, last_layer)
                here = both(wanted(layer_at, part), distance(layer, d) == h)
                if h == 0:
                    @pl.when(both(here, lax.rem(layer, 2) == c))
                    def _():
                        for core in range(2):
                            ring_copy(layer, part, d, core, core).start()
                        sib_copy(layer, part, d, True).start()
                else:
                    @pl.when(here)
                    def _():
                        ring_copy(layer, part, d, c, 0).wait_recv()
                        if h < YS - 1:
                            ring_copy(layer, part, d, c, 0).start()
                        sib_copy(layer, part, d, False).start()

    def need(layer, part):
        same = lax.div(layer, 2) == y

        @pl.when(jnp.logical_not(same))
        def _():
            for d in range(2):
                sib_wait(layer, part, d, False)

        @pl.when(both(same, lax.rem(layer, 2) != c))
        def _():
            for d in range(2):
                sib_wait(layer, part, d, True)

    def drain_weights(layer, part):
        for d in range(2):
            gap = distance(layer, d)

            @pl.when(both(gap == 0, lax.rem(layer, 2) == c))
            def _():
                for core in range(2):
                    ring_copy(layer, part, d, core, core).wait_send()
                sib_copy(layer, part, d, True).wait_send()

            @pl.when(both(gap > 0, gap < YS - 1))
            def _():
                ring_copy(layer, part, d, c, 0).wait_send()

            @pl.when(gap > 0)
            def _():
                sib_copy(layer, part, d, False).wait_send()

    feat_copy = remote(feat, xs.at[pl.ds(2, steps)], feat_sem.at[0], feat_sem.at[1], mine_to)
    feat_local = pltpu.make_async_copy(feat, xs.at[pl.ds(2, steps)], feat_sem.at[1])
    own_copy = remote(near, rows.at[1], tile_send.at[0], tile_recv.at[0], mine_to)
    own_local = pltpu.make_async_copy(near, rows.at[1], tile_recv.at[0])
    outer_copy = remote(near, rows.at[out_slot], tile_send.at[1], tile_recv.at[1], outer_to)
    outer_local = pltpu.make_async_copy(near, rows.at[2 * c], tile_recv.at[1])
    outer_land = remote(near, rows.at[2 * c], tile_send.at[1], tile_recv.at[1], outer_to)
    swap_copy = remote(rows.at[1], rows.at[2 * c], tile_send.at[2], tile_recv.at[2], sib)
    swap_land = remote(rows.at[1], rows.at[2 - 2 * c], tile_send.at[2], tile_recv.at[2], sib)

    point(-2, 0)

    @pl.when(native)
    def _():
        feat_local.start()
        own_local.start()

    @pl.when(jnp.logical_not(native))
    def _():
        feat_copy.start()
        own_copy.start()

    @pl.when(outer_native)
    def _():
        outer_local.start()

    @pl.when(both(out_valid, jnp.logical_not(outer_native)))
    def _():
        outer_copy.start()

    point(-2, 1)
    point(-2, 2)
    point(-1, 0)

    def halo(l, t, which):
        own = hb.at[l, t, 2]
        if which == 0:
            return remote(own, hb.at[l, t, c], halo_send.at[l, t, 0], halo_recv.at[l, t, c], right)
        if which == 1:
            return remote(own, hb.at[l, t, c + 3], halo_send.at[l, t, 1], halo_recv.at[l, t, c], left)
        if which == 2:
            return remote(own, hb.at[l, t, 1 + 2 * c], halo_send.at[l, t, 2], halo_recv.at[l, t, 2], sib)
        return remote(
            hb.at[l, t, 1 + 2 * c], hb.at[l, t, 4 * c], halo_send.at[l, t, 3], halo_recv.at[l, t, 3], sib
        )

    def landed(l, t, slot, which):
        ref = hb.at[l, t, slot]
        remote(ref, ref, halo_send.at[l, t, 3], halo_recv.at[l, t, which], sib).wait_recv()

    def send_halo(l, t):
        @pl.when(has_right)
        def _():
            halo(l, t, 0).start()

        @pl.when(has_left)
        def _():
            halo(l, t, 1).start()

        halo(l, t, 2).start()

    def convolve(l, t):
        now = xs[2 + t]
        before = xs[1 + t - lax.rem(l, 2)]
        pre = jnp.dot(
            jnp.concatenate([before, now], axis=1), wc[l].reshape(2 * ch, 2 * ch), preferred_element_type=F32
        )
        gate = 0.5 * jnp.tanh(0.5 * pre[:, ch:]) + 0.5
        hb[l, t, 2] = (jnp.tanh(pre[:, :ch]) * gate).astype(BF16)

    @pl.when(native)
    def _():
        feat_local.wait()

    @pl.when(jnp.logical_not(native))
    def _():
        feat_copy.wait_recv()

    need(0, 0)
    for t in range(steps):
        convolve(0, t)
        send_halo(0, t)

    @pl.when(native)
    def _():
        own_local.wait()

    @pl.when(jnp.logical_not(native))
    def _():
        own_copy.wait_recv()

    swap_copy.start()

    @pl.when(outer_native)
    def _():
        outer_local.wait()

    @pl.when(both(in_valid, jnp.logical_not(outer_native)))
    def _():
        outer_land.wait_recv()

    point(-1, 1)
    point(-1, 2)
    swap_land.wait_recv()
    for e in range(2):
        mid = rows[1, e]
        one = jnp.concatenate([jnp.zeros((tile, tile), BF16), mid, jnp.zeros((tile, tile), BF16)], axis=1)
        hops[e * tile : (e + 1) * tile, :] = one
        for col in range(5):
            total = jnp.zeros((tile, tile), F32)
            for via in range(3):
                if 0 <= col - via < 3:
                    total = total + jnp.dot(
                        mid[:, via * tile : (via + 1) * tile],
                        rows[via, e, :, (col - via) * tile : (col - via + 1) * tile],
                        preferred_element_type=F32,
                    )
            hops[(2 + e) * tile : (3 + e) * tile, col * tile : (col + 1) * tile] = total.astype(BF16)

    @pl.loop(0, last_layer)
    def _(l):
        need(l, 1)
        need(l, 2)
        own = hb[l, :, 2].reshape(steps * tile, ch)
        tot[...] += jnp.dot(own, wm[l, 0:4].reshape(ch, ch), preferred_element_type=F32)
        base[...] = xs[2:].reshape(steps * tile, ch).astype(F32) + jnp.dot(
            own, wm[l, 4:8].reshape(ch, ch), preferred_element_type=F32
        )
        for t in range(steps):
            @pl.when(outer_ok)
            def _():
                landed(l, t, 1 + 2 * c, 1 - c)
                halo(l, t, 3).start()
                landed(l, t, 4 * c, c)

            point(l, t)
            landed(l, t, 3 - 2 * c, 2)

            @pl.when(inner_ok)
            def _():
                landed(l, t, 4 - 4 * c, 3)

            fields = jnp.dot(hops[...], hb[l, t].reshape(5 * tile, ch), preferred_element_type=F32).astype(BF16)
            wide = jnp.concatenate([fields[i * tile : (i + 1) * tile] for i in range(4)], axis=1)
            mixed = base[t * tile : (t + 1) * tile] + jnp.dot(
                wide, wm[l, 8:24].reshape(4 * ch, ch), preferred_element_type=F32
            )
            xs[2 + t] = mixed.astype(BF16)
            if t == 0:
                need(l + 1, 0)
            convolve(l + 1, t)

            @pl.when(l < last_layer - 1)
            def _():
                send_halo(l + 1, t)

    need(last_layer, 1)
    own = hb[last_layer, :, 2].reshape(steps * tile, ch)
    result = tot[...] + jnp.dot(own, wm[last_layer, 0:4].reshape(ch, ch), preferred_element_type=F32)
    obuf[...] = result.astype(BF16).reshape(obuf.shape)

    def out_copy(section):
        return remote(obuf.at[:, section], out.at[m], out_send.at[section], out_recv.at[m], device(section, r))

    def out_local(section):
        return pltpu.make_async_copy(obuf.at[:, section], out.at[m], out_recv.at[m])

    for section in range(layers):
        keep = both(at_home, s == section)

        @pl.when(keep)
        def _():
            out_local(section).start()

        @pl.when(jnp.logical_not(keep))
        def _():
            out_copy(section).start()

    @pl.when(jnp.logical_not(native))
    def _():
        feat_copy.wait_send()
        own_copy.wait_send()

    @pl.when(both(out_valid, jnp.logical_not(outer_native)))
    def _():
        outer_copy.wait_send()

    swap_copy.wait_send()

    @pl.loop(0, last_layer)
    def _(l):
        for t in range(steps):
            @pl.when(has_right)
            def _():
                halo(l, t, 0).wait_send()

            @pl.when(has_left)
            def _():
                halo(l, t, 1).wait_send()

            halo(l, t, 2).wait_send()

            @pl.when(outer_ok)
            def _():
                halo(l, t, 3).wait_send()

        for part in range(3):
            drain_weights(l, part)

    for part in range(2):
        drain_weights(last_layer, part)

    for section in range(layers):
        @pl.when(jnp.logical_not(both(at_home, s == section)))
        def _():
            out_copy(section).wait_send()

    for sample in range(layers):
        keep = both(at_home, m == sample)
        ref = out.at[sample]

        @pl.when(keep)
        def _():
            pltpu.make_async_copy(obuf.at[:, sample], ref, out_recv.at[sample]).wait()

        @pl.when(jnp.logical_not(keep))
        def _():
            remote(obuf.at[:, sample], ref, out_send.at[sample], out_recv.at[sample], sib).wait_recv()


def body(
    features_in,
    filter_gate,
    self_mix,
    hop_one_mix,
    hop_two_mix,
    skip_weight,
    tile_values,
    tile_columns,
    tile_counts,
):
    micro, tile, steps, ch = features_in.shape
    layers = lax.axis_size("section")
    blocks = lax.axis_size("node")
    part = ch // 4
    feat = lax.dynamic_index_in_dim(features_in, lax.axis_index("section"), 0, keepdims=False)
    feat = feat.transpose(1, 0, 2)
    dma = pltpu.SemaphoreType.DMA
    anywhere = pl.BlockSpec(memory_space=pl.ANY)
    in_vmem = pl.BlockSpec(memory_space=pltpu.VMEM)
    in_smem = pl.BlockSpec(memory_space=pltpu.SMEM)
    landed = pl.pallas_call(
        functools.partial(kernel, layers, blocks),
        out_shape=jax.ShapeDtypeStruct((micro, steps, tile // layers, ch), BF16),
        in_specs=[anywhere] * 6 + [in_vmem, in_smem, in_smem],
        out_specs=anywhere,
        scratch_shapes=[
            pltpu.VMEM((2 + steps, tile, ch), BF16),
            pltpu.VMEM((layers, steps, 5, tile, ch), BF16),
            pltpu.VMEM((layers, 4, ch // 2, 2 * ch), BF16),
            pltpu.VMEM((layers, 24, part, ch), BF16),
            pltpu.VMEM((2, tile, 3 * tile), BF16),
            pltpu.VMEM((3, 2, tile, 3 * tile), BF16),
            pltpu.VMEM((4 * tile, 5 * tile), BF16),
            pltpu.VMEM((steps * tile, ch), F32),
            pltpu.VMEM((steps * tile, ch), F32),
            pltpu.VMEM((steps, layers, tile // layers, ch), BF16),
            dma((5,)),
            dma((2,)),
            dma((3,)),
            dma((3,)),
            dma((layers - 1, steps, 4)),
            dma((layers - 1, steps, 4)),
            dma((layers, 3, 2, 3)),
            dma((layers, 3, 2)),
            dma((layers, 3, 2)),
            dma((layers,)),
            dma((layers,)),
        ],
        compiler_params=pltpu.CompilerParams(
            collective_id=0, has_side_effects=True, vmem_limit_bytes=44 * 1024 * 1024
        ),
        cost_estimate=pl.CostEstimate(flops=7_000_000_000, bytes_accessed=4_000_000, transcendentals=3_000_000),
    )(
        feat,
        filter_gate.reshape(4, ch // 2, 2 * ch),
        self_mix.reshape(4, part, ch),
        hop_one_mix.reshape(8, part, ch),
        hop_two_mix.reshape(8, part, ch),
        skip_weight.reshape(4, part, ch),
        tile_values[:, 0],
        tile_columns[:, 0],
        tile_counts,
    )
    return landed.transpose(0, 2, 1, 3).astype(F32)[:, None]


def solution(mesh):
    in_specs = (
        P(None, "node", None, None),
        P("section", None, None, None),
        P("section", None, None),
        P("section", None, None, None),
        P("section", None, None, None),
        P("section", None, None),
        P(None, "node", None, None, None),
        P(None, "node", None),
        P(None, "node"),
    )
    out_specs = P(None, "node", "section", None, None)
    return jax.shard_map(body, mesh=mesh, in_specs=in_specs, out_specs=out_specs, check_vma=False)
```

time: 315 us -> 133 us (0.42); the launches traced: 310 us -> 133 us
  Pallas kernels: 0 us -> 124 us
  starting transfers between devices: 103 us -> 0 us
  waiting for transfers between devices: 76 us -> 0 us
  matrix products: 65.7 us -> 0 us
  local copies, waits for them, and re-layouts: 25.7 us -> 7.78 us
  blocking collectives: 17.5 us -> 0 us
  between operations: 15.1 us -> 0.03 us
  other arithmetic: 6.3 us -> 0.79 us
    pallas_call x0 -> x1, Pallas kernels: none -> 124 us  [body(): pl.pallas_call(functools.partial(kernel, layers, blocks), out_shape=jax.S...]
    ppermute x30 -> x0, starting transfers between devices: 103 us -> none  [moved(): lax.ppermute(value, 'node', [(source, source + steps) for source in range...]
    dot_general x60 -> x0, matrix products: 65.7 us -> none  [the longest x28 31.5 us: body(): jnp.dot(hopped[:, k].reshape(-1, channels), mix[(1 + k) * channels:(2 + k...]
    all_gather x2 -> x0, waiting for transfers between devices: 44.1 us -> none  [the longest x1 25.6 us: body(): lax.all_gather(filter_gate.reshape(1, 2 * channels, -1), 'section', tiled...]
    ppermute x30 -> x0, waiting for transfers between devices: 31.1 us -> none  [moved(): lax.ppermute(value, 'node', [(source, source + steps) for source in range...]
    all_to_all x1 -> x0, blocking collectives: 17.5 us -> none  [body(): lax.all_to_all(out.reshape(lax.axis_size('section'), -1, steps_len, chann...]
    slice x15 -> x0, local copies, waits for them, and re-layouts: 9.6 us -> none  [the longest x7 9.49 us: body(): hopped[:, k].reshape(-1, channels)]
    unnamed x73 -> x17, local copies, waits for them, and re-layouts: 12 us -> 7.77 us
  transfers between devices with their start and end apart: 32 -> 0, of which waited for: 11 -> 0; matrix products, arithmetic and copies ran while one was open for 9% -> 0% of each run, Pallas kernels for 0% -> 0%
where the time goes in v2:
time: 133 us
  Pallas kernels  124 us (93%)
  local copies, waits for them, and re-layouts  7.78 us (6%)
    pallas_call x1, Pallas kernels, body(): pl.pallas_call(functools.partial(kernel, layers, blocks), out_shape=jax.S...  124 us
    unnamed x17, local copies, waits for them, and re-layouts  7.77 us

profile of v2, /device:TPU:121, one launch (start us, length us, event | category | flops | bytes accessed | tf_op | source)
XLA Modules:
  0.0 133.0 jit_solution(16378512270902053904)
XLA Ops:
  0.0 0.0 copy-start
  0.0 0.9 copy.10.counts
  0.9 0.6 copy-done
  1.4 0.0 copy-start.1
  1.5 1.0 copy-done.1
  2.5 0.0 copy-start.2
  2.5 0.9 copy-done.2
  3.4 0.0 copy-start.3
  3.4 0.9 copy-done.3
  4.4 0.0 copy-start.4
  4.4 0.9 copy-done.4
  5.3 0.0 copy-start.5
  5.3 0.9 copy-done.5
  6.2 0.0 copy-start.6
  6.2 0.9 copy-done.6
  7.1 0.0 copy-start.7
  7.1 0.7 copy-done.7
  7.8 124.4 %shard_map.91 = bf16[8,3,16,256]{3,2,1,0:T(8,128)(2,1)S(1)} custom-call(bf16[3,128,256]{2,1,0:T(8,128)(2,1)S(1)} %dynamic-slice_bitcast_fusion.feat, bf16[4,128,512]{2,1,0:T(8,128)(2,1)S(1)} %bitcast.17, bf16[4,64,256]{2,1,0:T(8,128)(2,1)S(1)} %bitcast.21, bf16[8,64,256]{2,1,0:T(8,128)(2,1)S(1)} %bitcast.18, bf16[8,64,256]{2,1,0:T(8,128)(2,1)S(1)} %bitcast.19, ...), custom_call_target="tpu_custom_call" | custom-call | flops 7000000000 | bytes 4000000 | tf_op jit(solution)/shard_map/pallas_call | solution.py:527
  132.2 0.8 convert_bitcast_fusion
  (1 shorter events, 0.0 us)
Async XLA Ops:
  0.0 1.4 %copy-start = (bf16[8,128,3,256]{3,1,2,0:T(8,128)(2,1)S(1)}, bf16[8,128,3,256]{3,1,2,0:T(8,128)(2,1)}, u32[]{:S(2)}) copy-start(bf16[8,128,3,256]{3,1,2,0:T(8,128)(2,1)} %param.9) | copy-start | bytes 4718596
  1.4 1.0 copy-start.1
  2.5 0.9 copy-start.2
  3.4 0.9 copy-start.3
  4.4 0.9 copy-start.4
  5.3 0.9 copy-start.5
  6.2 0.9 copy-start.6
  7.1 0.7 copy-start.7

commit v3 on v2

--- a/solution.py
+++ b/solution.py
@@ -12,7 +12,9 @@
 MESH = pl.DeviceIdType.MESH
 XS = 4
 YS = 4
-LOOK = 6
+CONV_AHEAD = (14, 11, 6, 3)
+MIX_AHEAD = (25, 18, 10, 5, 1)
+START = max(CONV_AHEAD + MIX_AHEAD)
 
 
 def both(*conds):
@@ -54,10 +56,12 @@
     w_send,
     w_recv,
     w_sib,
+    w_side,
+    w_sib_side,
     out_send,
     out_recv,
 ):
-    steps, tile, ch = feat.shape
+    _, steps, tile, ch = feat.shape
     last_layer = layers - 1
     s = lax.axis_index("section")
     n = lax.axis_index("node")
@@ -98,6 +102,8 @@
     inner_ok = jnp.where(c == 0, has_right, has_left)
     outer_k = jnp.clip(k - 1 + 2 * c, 0, last)
     ring = [lax.rem(y + 1, YS), lax.rem(y + YS - 1, YS)]
+    column = lax.rem(x, 2)
+    partner = device(s, n + 1 - 2 * column)
 
     at_home = n == r
     native = both(s == m, at_home)
@@ -128,6 +134,7 @@
         pl.semaphore_signal(barrier, inc=1, device_id=dev, device_id_type=MESH)
 
     greet(sib)
+    greet(partner)
     for near_y in ring:
         for core in range(2):
             greet(device(2 * near_y + core, n))
@@ -179,7 +186,7 @@
 
     as_int = lambda cond: cond.astype(jnp.int32)
     expected = (
-        1
+        2
         + 4
         + as_int(has_right)
         + as_int(has_left)
@@ -193,88 +200,120 @@
     for load in loads:
         load.wait()
 
-    def piece(layer, part, first, count):
-        if part == 0:
-            return wc.at[layer, pl.ds(first, count)]
-        return wm.at[layer, pl.ds(12 * (part - 1) + 3 * first, 3 * count)]
-
-    def ring_copy(layer, part, d, core, slot):
-        ref = piece(layer, part, 2 * d + core, 1)
+    def conv_part(layer, first, count):
+        return wc.at[layer, pl.ds(first, count)]
+
+    def mix_part(layer, first, count):
+        return wm.at[layer, pl.ds(3 * first, 3 * count)]
+
+    def share(layer, kind, d, core):
+        return conv_part(layer, 2 * d + core, 1) if kind == 0 else mix_part(layer, 4 * d + 2 * core + column, 1)
+
+    def ring_copy(layer, kind, d, core, slot):
+        ref = share(layer, kind, d, core)
         return remote(
-            ref, ref, w_send.at[layer, part, d, slot], w_recv.at[layer, part, d], device(2 * ring[d] + core, n)
+            ref, ref, w_send.at[layer, kind, d, slot], w_recv.at[layer, kind, d], device(2 * ring[d] + core, n)
         )
 
-    def sib_copy(layer, part, d, whole):
-        ref = piece(layer, part, 2 * d, 2) if whole else piece(layer, part, 2 * d + c, 1)
-        return remote(ref, ref, w_send.at[layer, part, d, 2], w_sib.at[layer, part, d], sib)
-
-    def sib_wait(layer, part, d, whole):
-        ref = piece(layer, part, 2 * d, 2) if whole else piece(layer, part, 2 * d + 1 - c, 1)
-        remote(ref, ref, w_send.at[layer, part, d, 2], w_sib.at[layer, part, d], sib).wait_recv()
+    def whole_copy(layer, kind, d):
+        ref = conv_part(layer, 2 * d, 2) if kind == 0 else mix_part(layer, 4 * d, 4)
+        return remote(ref, ref, w_send.at[layer, kind, d, 2], w_sib.at[layer, kind, d], sib)
+
+    def sib_copy(layer, kind, d, core):
+        ref = share(layer, kind, d, core)
+        return remote(ref, ref, w_send.at[layer, kind, d, 2], w_sib.at[layer, kind, d], sib)
+
+    def side_copy(layer, d, from_column):
+        ref = mix_part(layer, 4 * d + 2 * c + from_column, 1)
+        return remote(ref, ref, w_send.at[layer, 1, d, 1], w_side.at[layer, d], partner)
+
+    def side_sib(layer, d, core):
+        ref = mix_part(layer, 4 * d + 2 * core + 1 - column, 1)
+        return remote(ref, ref, w_send.at[layer, 1, d, 3], w_sib_side.at[layer, d], sib)
 
     def distance(layer, d):
         gap = y - lax.div(layer, 2) if d == 0 else lax.div(layer, 2) - y
         return lax.rem(gap + YS, YS)
 
-    def wanted(layer, part):
-        valid = both(layer >= 0, layer < layers)
-        return both(valid, layer < last_layer) if part == 2 else valid
+    def deal(layer, kind, h, d, valid):
+        if h == YS:
+            @pl.when(both(valid, distance(layer, d) > 0))
+            def _():
+                side_copy(layer, d, 1 - column).wait_recv()
+                side_sib(layer, d, c).start()
+        elif h == 0:
+            @pl.when(both(valid, distance(layer, d) == 0, lax.rem(layer, 2) == c))
+            def _():
+                for core in range(2):
+                    ring_copy(layer, kind, d, core, core).start()
+                whole_copy(layer, kind, d).start()
+        else:
+            @pl.when(both(valid, distance(layer, d) == h))
+            def _():
+                ring_copy(layer, kind, d, c, 0).wait_recv()
+                if h < YS - 1:
+                    ring_copy(layer, kind, d, c, 0).start()
+                if kind == 1:
+                    side_copy(layer, d, column).start()
+                sib_copy(layer, kind, d, c).start()
+
+    events = [(kind, h, ahead) for kind, table in ((0, CONV_AHEAD), (1, MIX_AHEAD)) for h, ahead in enumerate(table)]
+    events.sort(key=lambda event: (event[1] > 0, event[2]))
 
     def point(l, t):
-        for d in range(2):
-            for h in range(YS):
-                at = t + LOOK - h
-                part = at % 3
-                layer_at = l + at // 3
-                layer = jnp.clip(layer_at, 0, last_layer)
-                here = both(wanted(layer_at, part), distance(layer, d) == h)
-                if h == 0:
-                    @pl.when(both(here, lax.rem(layer, 2) == c))
-                    def _():
-                        for core in range(2):
-                            ring_copy(layer, part, d, core, core).start()
-                        sib_copy(layer, part, d, True).start()
-                else:
-                    @pl.when(here)
-                    def _():
-                        ring_copy(layer, part, d, c, 0).wait_recv()
-                        if h < YS - 1:
-                            ring_copy(layer, part, d, c, 0).start()
-                        sib_copy(layer, part, d, False).start()
-
-    def need(layer, part):
+        for kind, h, ahead in events:
+            if (t + ahead) % 3 == 0:
+                layer = l + (t + ahead) // 3
+                for d in range(2):
+                    deal(jnp.minimum(layer, last_layer), kind, h, d, layer <= last_layer)
+
+    def before(first, stop):
+        for step in range(first, stop):
+            for kind, h, ahead in events:
+                if (step + ahead) % 3 == 0 and 0 <= step + ahead < 3 * layers:
+                    for d in range(2):
+                        deal(jnp.int32((step + ahead) // 3), kind, h, d, jnp.bool_(True))
+
+    def need(layer, kind):
         same = lax.div(layer, 2) == y
 
         @pl.when(jnp.logical_not(same))
         def _():
             for d in range(2):
-                sib_wait(layer, part, d, False)
+                sib_copy(layer, kind, d, 1 - c).wait_recv()
+                if kind == 1:
+                    side_sib(layer, d, 1 - c).wait_recv()
 
         @pl.when(both(same, lax.rem(layer, 2) != c))
         def _():
             for d in range(2):
-                sib_wait(layer, part, d, True)
-
-    def drain_weights(layer, part):
-        for d in range(2):
-            gap = distance(layer, d)
-
-            @pl.when(both(gap == 0, lax.rem(layer, 2) == c))
-            def _():
-                for core in range(2):
-                    ring_copy(layer, part, d, core, core).wait_send()
-                sib_copy(layer, part, d, True).wait_send()
-
-            @pl.when(both(gap > 0, gap < YS - 1))
-            def _():
-                ring_copy(layer, part, d, c, 0).wait_send()
-
-            @pl.when(gap > 0)
-            def _():
-                sib_copy(layer, part, d, False).wait_send()
-
-    feat_copy = remote(feat, xs.at[pl.ds(2, steps)], feat_sem.at[0], feat_sem.at[1], mine_to)
-    feat_local = pltpu.make_async_copy(feat, xs.at[pl.ds(2, steps)], feat_sem.at[1])
+                whole_copy(layer, kind, d).wait_recv()
+
+    def drain_weights(layer):
+        for kind in range(2):
+            for d in range(2):
+                gap = distance(layer, d)
+
+                @pl.when(both(gap == 0, lax.rem(layer, 2) == c))
+                def _():
+                    for core in range(2):
+                        ring_copy(layer, kind, d, core, core).wait_send()
+                    whole_copy(layer, kind, d).wait_send()
+
+                @pl.when(both(gap > 0, gap < YS - 1))
+                def _():
+                    ring_copy(layer, kind, d, c, 0).wait_send()
+
+                @pl.when(gap > 0)
+                def _():
+                    sib_copy(layer, kind, d, c).wait_send()
+                    if kind == 1:
+                        side_copy(layer, d, column).wait_send()
+                        side_sib(layer, d, c).wait_send()
+
+    mine = feat.at[s]
+    feat_copy = remote(mine, xs.at[pl.ds(2, steps)], feat_sem.at[0], feat_sem.at[1], mine_to)
+    feat_local = pltpu.make_async_copy(mine, xs.at[pl.ds(2, steps)], feat_sem.at[1])
     own_copy = remote(near, rows.at[1], tile_send.at[0], tile_recv.at[0], mine_to)
     own_local = pltpu.make_async_copy(near, rows.at[1], tile_recv.at[0])
     outer_copy = remote(near, rows.at[out_slot], tile_send.at[1], tile_recv.at[1], outer_to)
@@ -283,7 +322,7 @@
     swap_copy = remote(rows.at[1], rows.at[2 * c], tile_send.at[2], tile_recv.at[2], sib)
     swap_land = remote(rows.at[1], rows.at[2 - 2 * c], tile_send.at[2], tile_recv.at[2], sib)
 
-    point(-2, 0)
+    before(-START, 1 - CONV_AHEAD[0])
 
     @pl.when(native)
     def _():
@@ -303,9 +342,7 @@
     def _():
         outer_copy.start()
 
-    point(-2, 1)
-    point(-2, 2)
-    point(-1, 0)
+    before(1 - CONV_AHEAD[0], 1 - CONV_AHEAD[3])
 
     def halo(l, t, which):
         own = hb.at[l, t, 2]
@@ -374,8 +411,7 @@
     def _():
         outer_land.wait_recv()
 
-    point(-1, 1)
-    point(-1, 2)
+    before(1 - CONV_AHEAD[3], 0)
     swap_land.wait_recv()
     for e in range(2):
         mid = rows[1, e]
@@ -395,7 +431,6 @@
     @pl.loop(0, last_layer)
     def _(l):
         need(l, 1)
-        need(l, 2)
         own = hb[l, :, 2].reshape(steps * tile, ch)
         tot[...] += jnp.dot(own, wm[l, 0:4].reshape(ch, ch), preferred_element_type=F32)
         base[...] = xs[2:].reshape(steps * tile, ch).astype(F32) + jnp.dot(
@@ -479,11 +514,9 @@
             def _():
                 halo(l, t, 3).wait_send()
 
-        for part in range(3):
-            drain_weights(l, part)
-
-    for part in range(2):
-        drain_weights(last_layer, part)
+        drain_weights(l)
+
+    drain_weights(last_layer)
 
     for section in range(layers):
         @pl.when(jnp.logical_not(both(at_home, s == section)))
@@ -518,17 +551,16 @@
     layers = lax.axis_size("section")
     blocks = lax.axis_size("node")
     part = ch // 4
-    feat = lax.dynamic_index_in_dim(features_in, lax.axis_index("section"), 0, keepdims=False)
-    feat = feat.transpose(1, 0, 2)
+    feat = features_in.transpose(0, 2, 1, 3)
     dma = pltpu.SemaphoreType.DMA
-    anywhere = pl.BlockSpec(memory_space=pl.ANY)
+    in_hbm = pl.BlockSpec(memory_space=pltpu.HBM)
     in_vmem = pl.BlockSpec(memory_space=pltpu.VMEM)
     in_smem = pl.BlockSpec(memory_space=pltpu.SMEM)
     landed = pl.pallas_call(
         functools.partial(kernel, layers, blocks),
         out_shape=jax.ShapeDtypeStruct((micro, steps, tile // layers, ch), BF16),
-        in_specs=[anywhere] * 6 + [in_vmem, in_smem, in_smem],
-        out_specs=anywhere,
+        in_specs=[in_hbm] * 6 + [in_vmem, in_smem, in_smem],
+        out_specs=in_hbm,
         scratch_shapes=[
             pltpu.VMEM((2 + steps, tile, ch), BF16),
             pltpu.VMEM((layers, steps, 5, tile, ch), BF16),
@@ -546,14 +578,16 @@
             dma((3,)),
             dma((layers - 1, steps, 4)),
             dma((layers - 1, steps, 4)),
-            dma((layers, 3, 2, 3)),
-            dma((layers, 3, 2)),
-            dma((layers, 3, 2)),
+            dma((layers, 2, 2, 4)),
+            dma((layers, 2, 2)),
+            dma((layers, 2, 2)),
+            dma((layers, 2)),
+            dma((layers, 2)),
             dma((layers,)),
             dma((layers,)),
         ],
         compiler_params=pltpu.CompilerParams(
-            collective_id=0, has_side_effects=True, vmem_limit_bytes=44 * 1024 * 1024
+            collective_id=0, has_side_effects=True, vmem_limit_bytes=62 * 1024 * 1024
         ),
         cost_estimate=pl.CostEstimate(flops=7_000_000_000, bytes_accessed=4_000_000, transcendentals=3_000_000),
     )(

time: 133 us -> 91.6 us (0.69)
  Pallas kernels: 124 us -> 88.1 us
  local copies, waits for them, and re-layouts: 7.78 us -> 1.3 us
    pallas_call x1, Pallas kernels: 124 us -> 88.1 us  [body(): pl.pallas_call(functools.partial(kernel, layers, blocks), out_shape=jax.S...]
    unnamed x17 -> x1, local copies, waits for them, and re-layouts: 7.77 us -> 1.3 us
where the time goes in v3:
time: 91.6 us; the launch traced here: 91.1 us
  Pallas kernels  88.1 us (96%)
  other arithmetic  1.71 us (2%)
  local copies, waits for them, and re-layouts  1.3 us (1%)
    pallas_call x1, Pallas kernels, body(): pl.pallas_call(functools.partial(kernel, layers, blocks), out_shape=jax.S...  88.1 us

profile of v3, /device:TPU:121, one launch (start us, length us, event | category | flops | bytes accessed | tf_op | source)
XLA Modules:
  0.0 91.1 jit_solution(3591053852378290861)
XLA Ops:
  0.0 1.3 %copy.10.counts = s32[2,1]{1,0:T(2,128)} copy(s32[2,1]{0,1:T(1,128)} %param.17) | data formatting | bytes 16 | tf_op args[8]
  1.3 88.1 %shard_map.91 = bf16[8,3,16,256]{3,2,1,0:T(8,128)(2,1)} custom-call(bf16[8,3,128,256]{3,2,1,0:T(8,128)(2,1)} %bitcast.14, bf16[4,128,512]{2,1,0:T(8,128)(2,1)} %bitcast.15, bf16[4,64,256]{2,1,0:T(8,128)(2,1)} %bitcast.19, bf16[8,64,256]{2,1,0:T(8,128)(2,1)} %bitcast.16, bf16[8,64,256]{2,1,0:T(8,128)(2,1)} %bitcast.17, bf16[4,64,256]{2,1,0:T(8,128)(2,1)} %bitcast.20, ...), custom_call_target="tpu_custom_call" | custom-call | flops 7000000000 | bytes 4000000 | tf_op jit(solution)/shard_map/pallas_call | solution.py:559
  89.4 1.7 %convert_bitcast_fusion = f32[8,1,16,3,256]{4,2,3,1,0:T(8,128)} fusion(bf16[8,3,16,256]{3,2,1,0:T(8,128)(2,1)} %shard_map.91), kind=kLoop, calls=%fused_computation | loop fusion | flops 98304 | bytes 589824 | tf_op jit(solution)/shard_map/broadcast_in_dim | solution.py:604

commit v4 on v3

--- a/solution.py
+++ b/solution.py
@@ -12,9 +12,10 @@
 MESH = pl.DeviceIdType.MESH
 XS = 4
 YS = 4
-CONV_AHEAD = (14, 11, 6, 3)
-MIX_AHEAD = (25, 18, 10, 5, 1)
+CONV_AHEAD = (15, 10, 4)
+MIX_AHEAD = (15, 9, 3)
 START = max(CONV_AHEAD + MIX_AHEAD)
+SHARED = 8
 
 
 def both(*conds):
@@ -44,6 +45,8 @@
     near,
     rows,
     hops,
+    near_hops,
+    far_hops,
     base,
     tot,
     obuf,
@@ -51,13 +54,14 @@
     feat_sem,
     tile_send,
     tile_recv,
+    plane_send,
+    plane_recv,
     halo_send,
     halo_recv,
     w_send,
     w_recv,
+    w_quad,
     w_sib,
-    w_side,
-    w_sib_side,
     out_send,
     out_recv,
 ):
@@ -101,9 +105,16 @@
     outer_ok = jnp.where(c == 0, has_left, has_right)
     inner_ok = jnp.where(c == 0, has_right, has_left)
     outer_k = jnp.clip(k - 1 + 2 * c, 0, last)
-    ring = [lax.rem(y + 1, YS), lax.rem(y + YS - 1, YS)]
-    column = lax.rem(x, 2)
-    partner = device(s, n + 1 - 2 * column)
+
+    zs = blocks // XS
+    odd_x = lax.rem(x, 2)
+    low_z = lax.rem(z + side, 2)
+    quad = odd_x + 2 * low_z
+    quad_x = x + 1 - 2 * odd_x
+    quad_z = lax.rem(z + 1 - 2 * low_z + zs, zs)
+    quad_devices = [device(s, XS * z + quad_x), device(s, XS * quad_z + x), device(s, XS * quad_z + quad_x)]
+    flip_x, flip_z = 1 - 2 * odd_x, 2 - 4 * low_z
+    quad_parts = [quad + flip_x, quad + flip_z, quad + flip_x + flip_z]
 
     at_home = n == r
     native = both(s == m, at_home)
@@ -134,10 +145,11 @@
         pl.semaphore_signal(barrier, inc=1, device_id=dev, device_id_type=MESH)
 
     greet(sib)
-    greet(partner)
-    for near_y in ring:
+    for friend in quad_devices:
+        greet(friend)
+    for step in range(1, YS):
         for core in range(2):
-            greet(device(2 * near_y + core, n))
+            greet(device(2 * lax.rem(y + step, YS) + core, n))
 
     @pl.when(outer_ok)
     def _():
@@ -163,13 +175,13 @@
             for slot in range(3):
                 weight = both(columns[e, slot] == n - 1 + w, slot < counts[e, 0]).astype(F32)
                 total = total + tiles[e, slot].astype(F32) * weight
-            near[e, :, w * tile : (w + 1) * tile] = total.astype(BF16)
+            near[:, e, :, w * tile : (w + 1) * tile] = total.astype(BF16).reshape(YS, tile // YS, tile)
     xs[0:2] = jnp.zeros((2, tile, ch), BF16)
     tot[...] = jnp.zeros_like(tot)
 
     @pl.when(jnp.logical_not(outer_ok))
     def _():
-        rows[2 * c] = jnp.zeros((2, tile, 3 * tile), BF16)
+        rows[2 * c] = jnp.zeros(near.shape, BF16)
 
         @pl.loop(0, last_layer)
         def _(layer):
@@ -186,8 +198,9 @@
 
     as_int = lambda cond: cond.astype(jnp.int32)
     expected = (
-        2
-        + 4
+        1
+        + 3
+        + 2 * (YS - 1)
         + as_int(has_right)
         + as_int(has_left)
         + 1
@@ -200,126 +213,147 @@
     for load in loads:
         load.wait()
 
-    def conv_part(layer, first, count):
-        return wc.at[layer, pl.ds(first, count)]
-
-    def mix_part(layer, first, count):
-        return wm.at[layer, pl.ds(3 * first, 3 * count)]
-
-    def share(layer, kind, d, core):
-        return conv_part(layer, 2 * d + core, 1) if kind == 0 else mix_part(layer, 4 * d + 2 * core + column, 1)
-
-    def ring_copy(layer, kind, d, core, slot):
-        ref = share(layer, kind, d, core)
+    def piece(layer, kind, first, count):
+        return wc.at[layer, pl.ds(first, count)] if kind == 0 else wm.at[layer, pl.ds(3 * first, 3 * count)]
+
+    others = [lax.rem(y + step, YS) for step in range(1, YS)]
+
+    def owner_copy(layer, kind, step, core, shared):
+        ref = piece(layer, kind, 4 * core + quad, 1) if shared else piece(layer, kind, 4 * core, 4)
         return remote(
-            ref, ref, w_send.at[layer, kind, d, slot], w_recv.at[layer, kind, d], device(2 * ring[d] + core, n)
-        )
-
-    def whole_copy(layer, kind, d):
-        ref = conv_part(layer, 2 * d, 2) if kind == 0 else mix_part(layer, 4 * d, 4)
-        return remote(ref, ref, w_send.at[layer, kind, d, 2], w_sib.at[layer, kind, d], sib)
-
-    def sib_copy(layer, kind, d, core):
-        ref = share(layer, kind, d, core)
-        return remote(ref, ref, w_send.at[layer, kind, d, 2], w_sib.at[layer, kind, d], sib)
-
-    def side_copy(layer, d, from_column):
-        ref = mix_part(layer, 4 * d + 2 * c + from_column, 1)
-        return remote(ref, ref, w_send.at[layer, 1, d, 1], w_side.at[layer, d], partner)
-
-    def side_sib(layer, d, core):
-        ref = mix_part(layer, 4 * d + 2 * core + 1 - column, 1)
-        return remote(ref, ref, w_send.at[layer, 1, d, 3], w_sib_side.at[layer, d], sib)
-
-    def distance(layer, d):
-        gap = y - lax.div(layer, 2) if d == 0 else lax.div(layer, 2) - y
-        return lax.rem(gap + YS, YS)
-
-    def deal(layer, kind, h, d, valid):
-        if h == YS:
-            @pl.when(both(valid, distance(layer, d) > 0))
-            def _():
-                side_copy(layer, d, 1 - column).wait_recv()
-                side_sib(layer, d, c).start()
-        elif h == 0:
-            @pl.when(both(valid, distance(layer, d) == 0, lax.rem(layer, 2) == c))
-            def _():
-                for core in range(2):
-                    ring_copy(layer, kind, d, core, core).start()
-                whole_copy(layer, kind, d).start()
+            ref,
+            ref,
+            w_send.at[layer, kind, 2 * step + core],
+            w_recv.at[layer, kind],
+            device(2 * others[step] + core, n),
+        )
+
+    def owner_land(layer, kind, shared):
+        ref = piece(layer, kind, 4 * c + quad, 1) if shared else piece(layer, kind, 4 * c, 4)
+        return remote(ref, ref, w_send.at[layer, kind, 0], w_recv.at[layer, kind], sib)
+
+    def quad_copy(layer, kind, i):
+        ref = piece(layer, kind, 4 * c + quad, 1)
+        return remote(ref, ref, w_send.at[layer, kind, i], w_quad.at[layer, kind, i], quad_devices[i])
+
+    def quad_land(layer, kind, i):
+        ref = piece(layer, kind, 4 * c + quad_parts[i], 1)
+        return remote(ref, ref, w_send.at[layer, kind, i], w_quad.at[layer, kind, i], sib)
+
+    def whole_copy(layer, kind):
+        ref = piece(layer, kind, 0, 8)
+        return remote(ref, ref, w_send.at[layer, kind, 6], w_sib.at[layer, kind], sib)
+
+    def half_copy(layer, kind, core):
+        ref = piece(layer, kind, 4 * core, 4)
+        return remote(ref, ref, w_send.at[layer, kind, 6], w_sib.at[layer, kind], sib)
+
+    def deal(layer, kind, stage, valid):
+        same = lax.div(layer, 2) == y
+        apart = both(valid, jnp.logical_not(same))
+        early = layer < SHARED
+        late = jnp.logical_not(early)
+        if stage == 0:
+            mine = both(valid, same, lax.rem(layer, 2) == c)
+            for shared, when in ((True, early), (False, late)):
+                @pl.when(both(mine, when))
+                def _():
+                    for step in (1, 0, 2):
+                        for core in range(2):
+                            owner_copy(layer, kind, step, core, shared).start()
+
+            @pl.when(mine)
+            def _():
+                whole_copy(layer, kind).start()
+        elif stage == 1:
+            @pl.when(both(apart, early))
+            def _():
+                owner_land(layer, kind, True).wait_recv()
+                for i in (2, 0, 1):
+                    quad_copy(layer, kind, i).start()
+
+            @pl.when(both(apart, late))
+            def _():
+                owner_land(layer, kind, False).wait_recv()
+                half_copy(layer, kind, c).start()
         else:
-            @pl.when(both(valid, distance(layer, d) == h))
-            def _():
-                ring_copy(layer, kind, d, c, 0).wait_recv()
-                if h < YS - 1:
-                    ring_copy(layer, kind, d, c, 0).start()
-                if kind == 1:
-                    side_copy(layer, d, column).start()
-                sib_copy(layer, kind, d, c).start()
-
-    events = [(kind, h, ahead) for kind, table in ((0, CONV_AHEAD), (1, MIX_AHEAD)) for h, ahead in enumerate(table)]
+            @pl.when(both(apart, early))
+            def _():
+                for i in range(3):
+                    quad_land(layer, kind, i).wait_recv()
+                half_copy(layer, kind, c).start()
+
+    events = [
+        (kind, stage, ahead) for kind, table in ((0, CONV_AHEAD), (1, MIX_AHEAD)) for stage, ahead in enumerate(table)
+    ]
     events.sort(key=lambda event: (event[1] > 0, event[2]))
 
     def point(l, t):
-        for kind, h, ahead in events:
+        for kind, stage, ahead in events:
             if (t + ahead) % 3 == 0:
                 layer = l + (t + ahead) // 3
-                for d in range(2):
-                    deal(jnp.minimum(layer, last_layer), kind, h, d, layer <= last_layer)
+                deal(jnp.minimum(layer, last_layer), kind, stage, layer <= last_layer)
 
     def before(first, stop):
         for step in range(first, stop):
-            for kind, h, ahead in events:
+            for kind, stage, ahead in events:
                 if (step + ahead) % 3 == 0 and 0 <= step + ahead < 3 * layers:
-                    for d in range(2):
-                        deal(jnp.int32((step + ahead) // 3), kind, h, d, jnp.bool_(True))
+                    deal(jnp.int32((step + ahead) // 3), kind, stage, jnp.bool_(True))
 
     def need(layer, kind):
         same = lax.div(layer, 2) == y
 
         @pl.when(jnp.logical_not(same))
         def _():
-            for d in range(2):
-                sib_copy(layer, kind, d, 1 - c).wait_recv()
-                if kind == 1:
-                    side_sib(layer, d, 1 - c).wait_recv()
+            half_copy(layer, kind, 1 - c).wait_recv()
 
         @pl.when(both(same, lax.rem(layer, 2) != c))
         def _():
-            for d in range(2):
-                whole_copy(layer, kind, d).wait_recv()
+            whole_copy(layer, kind).wait_recv()
 
     def drain_weights(layer):
+        same = lax.div(layer, 2) == y
+        early = layer < SHARED
         for kind in range(2):
-            for d in range(2):
-                gap = distance(layer, d)
-
-                @pl.when(both(gap == 0, lax.rem(layer, 2) == c))
+            for shared, when in ((True, early), (False, jnp.logical_not(early))):
+                @pl.when(both(same, lax.rem(layer, 2) == c, when))
                 def _():
-                    for core in range(2):
-                        ring_copy(layer, kind, d, core, core).wait_send()
-                    whole_copy(layer, kind, d).wait_send()
-
-                @pl.when(both(gap > 0, gap < YS - 1))
-                def _():
-                    ring_copy(layer, kind, d, c, 0).wait_send()
-
-                @pl.when(gap > 0)
-                def _():
-                    sib_copy(layer, kind, d, c).wait_send()
-                    if kind == 1:
-                        side_copy(layer, d, column).wait_send()
-                        side_sib(layer, d, c).wait_send()
+                    for step in range(YS - 1):
+                        for core in range(2):
+                            owner_copy(layer, kind, step, core, shared).wait_send()
+
+            @pl.when(both(same, lax.rem(layer, 2) == c))
+            def _():
+                whole_copy(layer, kind).wait_send()
+
+            @pl.when(both(jnp.logical_not(same), early))
+            def _():
+                for i in range(3):
+                    quad_copy(layer, kind, i).wait_send()
+
+            @pl.when(jnp.logical_not(same))
+            def _():
+                half_copy(layer, kind, c).wait_send()
 
     mine = feat.at[s]
     feat_copy = remote(mine, xs.at[pl.ds(2, steps)], feat_sem.at[0], feat_sem.at[1], mine_to)
     feat_local = pltpu.make_async_copy(mine, xs.at[pl.ds(2, steps)], feat_sem.at[1])
-    own_copy = remote(near, rows.at[1], tile_send.at[0], tile_recv.at[0], mine_to)
+    own_copy = remote(near.at[y], rows.at[1, y], tile_send.at[0], tile_recv.at[0], mine_to)
     own_local = pltpu.make_async_copy(near, rows.at[1], tile_recv.at[0])
-    outer_copy = remote(near, rows.at[out_slot], tile_send.at[1], tile_recv.at[1], outer_to)
+    outer_copy = remote(near.at[y], rows.at[out_slot, y], tile_send.at[1], tile_recv.at[1], outer_to)
     outer_local = pltpu.make_async_copy(near, rows.at[2 * c], tile_recv.at[1])
-    outer_land = remote(near, rows.at[2 * c], tile_send.at[1], tile_recv.at[1], outer_to)
+    outer_land = remote(near.at[y], rows.at[2 * c, y], tile_send.at[1], tile_recv.at[1], outer_to)
     swap_copy = remote(rows.at[1], rows.at[2 * c], tile_send.at[2], tile_recv.at[2], sib)
+    def plane_copy(slot, which, step):
+        ref = rows.at[slot, y]
+        return remote(
+            ref, ref, plane_send.at[which, step], plane_recv.at[which, step], device(2 * others[step] + c, n)
+        )
+
+    def plane_land(slot, which, step):
+        ref = rows.at[slot, others[YS - 2 - step]]
+        return remote(ref, ref, plane_send.at[which, step], plane_recv.at[which, step], sib)
+
     swap_land = remote(rows.at[1], rows.at[2 - 2 * c], tile_send.at[2], tile_recv.at[2], sib)
 
     before(-START, 1 - CONV_AHEAD[0])
@@ -342,7 +376,21 @@
     def _():
         outer_copy.start()
 
-    before(1 - CONV_AHEAD[0], 1 - CONV_AHEAD[3])
+    before(1 - CONV_AHEAD[0], 1 - CONV_AHEAD[1])
+
+    @pl.when(jnp.logical_not(native))
+    def _():
+        own_copy.wait_recv()
+        for step in range(YS - 1):
+            plane_copy(1, 0, step).start()
+
+    @pl.when(both(in_valid, jnp.logical_not(outer_native)))
+    def _():
+        outer_land.wait_recv()
+        for step in range(YS - 1):
+            plane_copy(2 * c, 1, step).start()
+
+    before(1 - CONV_AHEAD[1], 1 - CONV_AHEAD[2])
 
     def halo(l, t, which):
         own = hb.at[l, t, 2]
@@ -399,7 +447,8 @@
 
     @pl.when(jnp.logical_not(native))
     def _():
-        own_copy.wait_recv()
+        for step in range(YS - 1):
+            plane_land(1, 0, step).wait_recv()
 
     swap_copy.start()
 
@@ -409,24 +458,66 @@
 
     @pl.when(both(in_valid, jnp.logical_not(outer_native)))
     def _():
-        outer_land.wait_recv()
-
-    before(1 - CONV_AHEAD[3], 0)
+        for step in range(YS - 1):
+            plane_land(2 * c, 1, step).wait_recv()
+
+    before(1 - CONV_AHEAD[2], 0)
     swap_land.wait_recv()
     for e in range(2):
-        mid = rows[1, e]
-        one = jnp.concatenate([jnp.zeros((tile, tile), BF16), mid, jnp.zeros((tile, tile), BF16)], axis=1)
-        hops[e * tile : (e + 1) * tile, :] = one
+        mid = rows[1, :, e].reshape(tile, 3 * tile)
+        for col in range(5):
+            inside = mid[:, (col - 1) * tile : col * tile] if 0 < col < 4 else jnp.zeros((tile, tile), BF16)
+            hops[col, e * tile : (e + 1) * tile] = inside
         for col in range(5):
             total = jnp.zeros((tile, tile), F32)
             for via in range(3):
                 if 0 <= col - via < 3:
                     total = total + jnp.dot(
                         mid[:, via * tile : (via + 1) * tile],
-                        rows[via, e, :, (col - via) * tile : (col - via + 1) * tile],
+                        rows[via, :, e, :, (col - via) * tile : (col - via + 1) * tile].reshape(tile, tile),
                         preferred_element_type=F32,
                     )
-            hops[(2 + e) * tile : (3 + e) * tile, col * tile : (col + 1) * tile] = total.astype(BF16)
+            hops[col, (2 + e) * tile : (3 + e) * tile] = total.astype(BF16)
+    for i in range(4):
+        near_hops[:, i * tile : (i + 1) * tile] = hops[c + i]
+    far_hops[...] = hops[4 - 4 * c, 2 * tile :]
+
+    def hand_on(l, t):
+        @pl.when(outer_ok)
+        def _():
+            landed(l, t, 1 + 2 * c, 1 - c)
+            halo(l, t, 3).start()
+            landed(l, t, 4 * c, c)
+
+    def out_copy(section, t):
+        return remote(
+            obuf.at[t, section],
+            out.at[m, t],
+            out_send.at[section, t],
+            out_recv.at[m, t],
+            device(section, r),
+        )
+
+    def out_local(section, t, sample):
+        return pltpu.make_async_copy(obuf.at[t, section], out.at[sample, t], out_recv.at[sample, t])
+
+    def finish(t):
+        if t == 0:
+            need(last_layer, 1)
+        result = tot[t * tile : (t + 1) * tile] + jnp.dot(
+            hb[last_layer, t, 2], wm[last_layer, 0:4].reshape(ch, ch), preferred_element_type=F32
+        )
+        obuf[t] = result.astype(BF16).reshape(layers, tile // layers, ch)
+        for section in range(layers):
+            keep = both(at_home, s == section)
+
+            @pl.when(keep)
+            def _():
+                out_local(section, t, m).start()
+
+            @pl.when(jnp.logical_not(keep))
+            def _():
+                out_copy(section, t).start()
 
     @pl.loop(0, last_layer)
     def _(l):
@@ -436,25 +527,27 @@
         base[...] = xs[2:].reshape(steps * tile, ch).astype(F32) + jnp.dot(
             own, wm[l, 4:8].reshape(ch, ch), preferred_element_type=F32
         )
+        hand_on(l, 0)
         for t in range(steps):
-            @pl.when(outer_ok)
-            def _():
-                landed(l, t, 1 + 2 * c, 1 - c)
-                halo(l, t, 3).start()
-                landed(l, t, 4 * c, c)
-
-            point(l, t)
             landed(l, t, 3 - 2 * c, 2)
-
-            @pl.when(inner_ok)
-            def _():
-                landed(l, t, 4 - 4 * c, 3)
-
-            fields = jnp.dot(hops[...], hb[l, t].reshape(5 * tile, ch), preferred_element_type=F32).astype(BF16)
+            fields = jnp.dot(
+                near_hops[...], hb[l, t, pl.ds(c, 4)].reshape(4 * tile, ch), preferred_element_type=F32
+            ).astype(BF16)
             wide = jnp.concatenate([fields[i * tile : (i + 1) * tile] for i in range(4)], axis=1)
             mixed = base[t * tile : (t + 1) * tile] + jnp.dot(
                 wide, wm[l, 8:24].reshape(4 * ch, ch), preferred_element_type=F32
             )
+            if t < steps - 1:
+                hand_on(l, t + 1)
+            point(l, t)
+
+            @pl.when(inner_ok)
+            def _():
+                landed(l, t, 4 - 4 * c, 3)
+
+            fields = jnp.dot(far_hops[...], hb[l, t, 4 - 4 * c], preferred_element_type=F32).astype(BF16)
+            wide = jnp.concatenate([fields[:tile], fields[tile:]], axis=1)
+            mixed = mixed + jnp.dot(wide, wm[l, 16:24].reshape(2 * ch, ch), preferred_element_type=F32)
             xs[2 + t] = mixed.astype(BF16)
             if t == 0:
                 need(l + 1, 0)
@@ -464,36 +557,25 @@
             def _():
                 send_halo(l + 1, t)
 
-    need(last_layer, 1)
-    own = hb[last_layer, :, 2].reshape(steps * tile, ch)
-    result = tot[...] + jnp.dot(own, wm[last_layer, 0:4].reshape(ch, ch), preferred_element_type=F32)
-    obuf[...] = result.astype(BF16).reshape(obuf.shape)
-
-    def out_copy(section):
-        return remote(obuf.at[:, section], out.at[m], out_send.at[section], out_recv.at[m], device(section, r))
-
-    def out_local(section):
-        return pltpu.make_async_copy(obuf.at[:, section], out.at[m], out_recv.at[m])
-
-    for section in range(layers):
-        keep = both(at_home, s == section)
-
-        @pl.when(keep)
-        def _():
-            out_local(section).start()
-
-        @pl.when(jnp.logical_not(keep))
-        def _():
-            out_copy(section).start()
+            @pl.when(l == last_layer - 1)
+            def _():
+                finish(t)
 
     @pl.when(jnp.logical_not(native))
     def _():
         feat_copy.wait_send()
         own_copy.wait_send()
+        for step in range(YS - 1):
+            plane_copy(1, 0, step).wait_send()
 
     @pl.when(both(out_valid, jnp.logical_not(outer_native)))
     def _():
         outer_copy.wait_send()
+
+    @pl.when(both(in_valid, jnp.logical_not(outer_native)))
+    def _():
+        for step in range(YS - 1):
+            plane_copy(2 * c, 1, step).wait_send()
 
     swap_copy.wait_send()
 
@@ -521,19 +603,22 @@
     for section in range(layers):
         @pl.when(jnp.logical_not(both(at_home, s == section)))
         def _():
-            out_copy(section).wait_send()
+            for t in range(steps):
+                out_copy(section, t).wait_send()
 
     for sample in range(layers):
         keep = both(at_home, m == sample)
-        ref = out.at[sample]
 
         @pl.when(keep)
         def _():
-            pltpu.make_async_copy(obuf.at[:, sample], ref, out_recv.at[sample]).wait()
+            for t in range(steps):
+                out_local(s, t, sample).wait()
 
         @pl.when(jnp.logical_not(keep))
         def _():
-            remote(obuf.at[:, sample], ref, out_send.at[sample], out_recv.at[sample], sib).wait_recv()
+            for t in range(steps):
+                ref = out.at[sample, t]
+                remote(obuf.at[t, 0], ref, out_send.at[sample, t], out_recv.at[sample, t], sib).wait_recv()
 
 
 def body(
@@ -564,11 +649,13 @@
         scratch_shapes=[
             pltpu.VMEM((2 + steps, tile, ch), BF16),
             pltpu.VMEM((layers, steps, 5, tile, ch), BF16),
-            pltpu.VMEM((layers, 4, ch // 2, 2 * ch), BF16),
+            pltpu.VMEM((layers, 8, ch // 4, 2 * ch), BF16),
             pltpu.VMEM((layers, 24, part, ch), BF16),
-            pltpu.VMEM((2, tile, 3 * tile), BF16),
-            pltpu.VMEM((3, 2, tile, 3 * tile), BF16),
-            pltpu.VMEM((4 * tile, 5 * tile), BF16),
+            pltpu.VMEM((YS, 2, tile // YS, 3 * tile), BF16),
+            pltpu.VMEM((3, YS, 2, tile // YS, 3 * tile), BF16),
+            pltpu.VMEM((5, 4 * tile, tile), BF16),
+            pltpu.VMEM((4 * tile, 4 * tile), BF16),
+            pltpu.VMEM((2 * tile, tile), BF16),
             pltpu.VMEM((steps * tile, ch), F32),
             pltpu.VMEM((steps * tile, ch), F32),
             pltpu.VMEM((steps, layers, tile // layers, ch), BF16),
@@ -576,15 +663,16 @@
             dma((2,)),
             dma((3,)),
             dma((3,)),
+            dma((2, 3)),
+            dma((2, 3)),
             dma((layers - 1, steps, 4)),
             dma((layers - 1, steps, 4)),
-            dma((layers, 2, 2, 4)),
-            dma((layers, 2, 2)),
-            dma((layers, 2, 2)),
+            dma((layers, 2, 7)),
             dma((layers, 2)),
+            dma((layers, 2, 3)),
             dma((layers, 2)),
-            dma((layers,)),
-            dma((layers,)),
+            dma((layers, steps)),
+            dma((layers, steps)),
         ],
         compiler_params=pltpu.CompilerParams(
             collective_id=0, has_side_effects=True, vmem_limit_bytes=62 * 1024 * 1024
@@ -592,7 +680,7 @@
         cost_estimate=pl.CostEstimate(flops=7_000_000_000, bytes_accessed=4_000_000, transcendentals=3_000_000),
     )(
         feat,
-        filter_gate.reshape(4, ch // 2, 2 * ch),
+        filter_gate.reshape(8, ch // 4, 2 * ch),
         self_mix.reshape(4, part, ch),
         hop_one_mix.reshape(8, part, ch),
         hop_two_mix.reshape(8, part, ch),

time: 91.6 us -> 88.6 us (0.967)
  Pallas kernels: 88.1 us -> 85.5 us
    pallas_call x1, Pallas kernels: 88.1 us -> 85.5 us  [body(): pl.pallas_call(functools.partial(kernel, layers, blocks), out_shape=jax.S...]
where the time goes in v4:
time: 88.6 us; the launch traced here: 88.5 us
  Pallas kernels  85.5 us (97%)
  other arithmetic  1.71 us (2%)
  local copies, waits for them, and re-layouts  1.3 us (1%)
    pallas_call x1, Pallas kernels, body(): pl.pallas_call(functools.partial(kernel, layers, blocks), out_shape=jax.S...  85.5 us

profile of v4, /device:TPU:121, one launch (start us, length us, event | category | flops | bytes accessed | tf_op | source)
XLA Modules:
  0.0 88.5 jit_solution(7760201588491997131)
XLA Ops:
  0.0 1.3 %copy.10.counts = s32[2,1]{1,0:T(2,128)} copy(s32[2,1]{0,1:T(1,128)} %param.17) | data formatting | bytes 16 | tf_op args[8]
  1.3 85.5 %shard_map.91 = bf16[8,3,16,256]{3,2,1,0:T(8,128)(2,1)} custom-call(bf16[8,3,128,256]{3,2,1,0:T(8,128)(2,1)} %bitcast.14, bf16[8,64,512]{2,1,0:T(8,128)(2,1)} %bitcast.15, bf16[4,64,256]{2,1,0:T(8,128)(2,1)} %bitcast.19, bf16[8,64,256]{2,1,0:T(8,128)(2,1)} %bitcast.16, bf16[8,64,256]{2,1,0:T(8,128)(2,1)} %bitcast.17, bf16[4,64,256]{2,1,0:T(8,128)(2,1)} %bitcast.20, ...), custom_call_target="tpu_custom_call" | custom-call | flops 7000000000 | bytes 4000000 | tf_op jit(solution)/shard_map/pallas_call | solution.py:644
  86.8 1.7 %convert_bitcast_fusion = f32[8,1,16,3,256]{4,2,3,1,0:T(8,128)} fusion(bf16[8,3,16,256]{3,2,1,0:T(8,128)(2,1)} %shard_map.91), kind=kLoop, calls=%fused_computation | loop fusion | flops 98304 | bytes 589824 | tf_op jit(solution)/shard_map/broadcast_in_dim | solution.py:692

commit v5 on v4

--- a/solution.py
+++ b/solution.py
@@ -409,13 +409,17 @@
         remote(ref, ref, halo_send.at[l, t, 3], halo_recv.at[l, t, which], sib).wait_recv()
 
     def send_halo(l, t):
-        @pl.when(has_right)
+        @pl.when(both(has_right, c == 1))
         def _():
             halo(l, t, 0).start()
 
         @pl.when(has_left)
         def _():
             halo(l, t, 1).start()
+
+        @pl.when(both(has_right, c == 0))
+        def _():
+            halo(l, t, 0).start()
 
         halo(l, t, 2).start()
 
@@ -487,7 +491,6 @@
         def _():
             landed(l, t, 1 + 2 * c, 1 - c)
             halo(l, t, 3).start()
-            landed(l, t, 4 * c, c)
 
     def out_copy(section, t):
         return remote(
@@ -530,6 +533,11 @@
         hand_on(l, 0)
         for t in range(steps):
             landed(l, t, 3 - 2 * c, 2)
+
+            @pl.when(outer_ok)
+            def _():
+                landed(l, t, 4 * c, c)
+
             fields = jnp.dot(
                 near_hops[...], hb[l, t, pl.ds(c, 4)].reshape(4 * tile, ch), preferred_element_type=F32
             ).astype(BF16)
@@ -537,13 +545,14 @@
             mixed = base[t * tile : (t + 1) * tile] + jnp.dot(
                 wide, wm[l, 8:24].reshape(4 * ch, ch), preferred_element_type=F32
             )
+            point(l, t)
+
+            @pl.when(inner_ok)
+            def _():
+                landed(l, t, 4 - 4 * c, 3)
+
             if t < steps - 1:
                 hand_on(l, t + 1)
-            point(l, t)
-
-            @pl.when(inner_ok)
-            def _():
-                landed(l, t, 4 - 4 * c, 3)
 
             fields = jnp.dot(far_hops[...], hb[l, t, 4 - 4 * c], preferred_element_type=F32).astype(BF16)
             wide = jnp.concatenate([fields[:tile], fields[tile:]], axis=1)

time: 88.6 us -> 87.6 us (0.989)
  Pallas kernels: 85.5 us -> 84.3 us
    pallas_call x1, Pallas kernels: 85.5 us -> 84.3 us  [body(): pl.pallas_call(functools.partial(kernel, layers, blocks), out_shape=jax.S...]
where the time goes in v5:
time: 87.6 us; the launch traced here: 87.3 us
  Pallas kernels  84.3 us (96%)
  other arithmetic  1.71 us (2%)
  local copies, waits for them, and re-layouts  1.3 us (1%)
    pallas_call x1, Pallas kernels, body(): pl.pallas_call(functools.partial(kernel, layers, blocks), out_shape=jax.S...  84.3 us

profile of v5, /device:TPU:121, one launch (start us, length us, event | category | flops | bytes accessed | tf_op | source)
XLA Modules:
  0.0 87.3 jit_solution(11656238768742185783)
XLA Ops:
  0.0 1.3 %copy.10.counts = s32[2,1]{1,0:T(2,128)} copy(s32[2,1]{0,1:T(1,128)} %param.17) | data formatting | bytes 16 | tf_op args[8]
  1.3 84.3 %shard_map.91 = bf16[8,3,16,256]{3,2,1,0:T(8,128)(2,1)} custom-call(bf16[8,3,128,256]{3,2,1,0:T(8,128)(2,1)} %bitcast.14, bf16[8,64,512]{2,1,0:T(8,128)(2,1)} %bitcast.15, bf16[4,64,256]{2,1,0:T(8,128)(2,1)} %bitcast.19, bf16[8,64,256]{2,1,0:T(8,128)(2,1)} %bitcast.16, bf16[8,64,256]{2,1,0:T(8,128)(2,1)} %bitcast.17, bf16[4,64,256]{2,1,0:T(8,128)(2,1)} %bitcast.20, ...), custom_call_target="tpu_custom_call" | custom-call | flops 7000000000 | bytes 4000000 | tf_op jit(solution)/shard_map/pallas_call | solution.py:653
  85.6 1.7 %convert_bitcast_fusion = f32[8,1,16,3,256]{4,2,3,1,0:T(8,128)} fusion(bf16[8,3,16,256]{3,2,1,0:T(8,128)(2,1)} %shard_map.91), kind=kLoop, calls=%fused_computation | loop fusion | flops 98304 | bytes 589824 | tf_op jit(solution)/shard_map/broadcast_in_dim | solution.py:701

commit v6 on v5

--- a/solution.py
+++ b/solution.py
@@ -173,7 +173,7 @@
         for w in range(3):
             total = jnp.zeros((tile, tile), F32)
             for slot in range(3):
-                weight = both(columns[e, slot] == n - 1 + w, slot < counts[e, 0]).astype(F32)
+                weight = both(columns[e, slot] == n - 1 + w, slot < counts[e]).astype(F32)
                 total = total + tiles[e, slot].astype(F32) * weight
             near[:, e, :, w * tile : (w + 1) * tile] = total.astype(BF16).reshape(YS, tile // YS, tile)
     xs[0:2] = jnp.zeros((2, tile, ch), BF16)
@@ -696,7 +696,7 @@
         skip_weight.reshape(4, part, ch),
         tile_values[:, 0],
         tile_columns[:, 0],
-        tile_counts,
+        tile_counts[:, 0],
     )
     return landed.transpose(0, 2, 1, 3).astype(F32)[:, None]
 

time: 87.6 us -> 86.3 us (0.985)
  local copies, waits for them, and re-layouts: 1.3 us -> 0 us
    unnamed x1 -> x0, local copies, waits for them, and re-layouts: 1.3 us -> none
where the time goes in v6:
time: 86.3 us; the launch traced here: 86 us
  Pallas kernels  84.3 us (98%)
  other arithmetic  1.71 us (2%)
    pallas_call x1, Pallas kernels, body(): pl.pallas_call(functools.partial(kernel, layers, blocks), out_shape=jax.S...  84.3 us

profile of v6, /device:TPU:121, one launch (start us, length us, event | category | flops | bytes accessed | tf_op | source)
XLA Modules:
  0.0 86.0 jit_solution(11022355471375434866)
XLA Ops:
  0.0 84.3 %shard_map.91 = bf16[8,3,16,256]{3,2,1,0:T(8,128)(2,1)} custom-call(bf16[8,3,128,256]{3,2,1,0:T(8,128)(2,1)} %bitcast.15, bf16[8,64,512]{2,1,0:T(8,128)(2,1)} %bitcast.16, bf16[4,64,256]{2,1,0:T(8,128)(2,1)} %bitcast.20, bf16[8,64,256]{2,1,0:T(8,128)(2,1)} %bitcast.17, bf16[8,64,256]{2,1,0:T(8,128)(2,1)} %bitcast.18, bf16[4,64,256]{2,1,0:T(8,128)(2,1)} %bitcast.21, ...), custom_call_target="tpu_custom_call" | custom-call | flops 7000000000 | bytes 4000000 | tf_op jit(solution)/shard_map/pallas_call | solution.py:653
  84.3 1.7 %convert_bitcast_fusion = f32[8,1,16,3,256]{4,2,3,1,0:T(8,128)} fusion(bf16[8,3,16,256]{3,2,1,0:T(8,128)(2,1)} %shard_map.91), kind=kLoop, calls=%fused_computation | loop fusion | flops 98304 | bytes 589824 | tf_op jit(solution)/shard_map/broadcast_in_dim | solution.py:701
